TPU v7x, 512 devices: a whole 4x4x16 slice. The times are simulated.
512 devices in a mesh: leaf: 512 (over y, x, z, core).
Axes of the slice: x: 4, y: 4, z: 16, core: 2. Of those that a mesh axis runs over, the one named last changes fastest.
Arguments:
- values: float32 [524288, 128], P('leaf'), may hold values from -6 to 6
- coords: float32 [3, 524288], P(None, 'leaf'), may hold values from 0 to 2.5, as said below
- permutation: int32 [524288], P('leaf'), may hold values from 0 to 524287, as said below
- basis: float32 [524288, 256], P('leaf'), may hold values from -0.1875 to 0.1875
- transfers: float32 [229376, 256], P('leaf'), may hold values from -0.375 to 0.375
- couplings: float32 [491520, 256], P('leaf'), may hold values from -0.375 to 0.375
- interactions: int32 [512, 4, 2], P('leaf'), may hold values from 0 to 511, as said below
Outputs:
- product: float32 [524288, 128], P('leaf')
Inputs may be any that keep to these rules, and one draw needn't show every extreme that they name: Within each aligned block of 1024 tree positions, a permutation of that block's indices. `interactions`: entries of level l lie below 512/2^l and are equal over each aligned group of 2^l leaves; each names a node at level l that differs from the leaf's own ancestor (leaf // 2^l) by 2 or 3 in either direction. `coords`: the first coordinate of a point of leaf d lies in [d % 2, d % 2 + 1.5); the others in [0, 1).
All inputs are finite; a program needn't handle non-finite values.
Results may differ from a plain program's by a relative error of at most 0.00017.
Values sent between devices are 32-bit elements; how exact they have to be, the bound alone decides.
A program may use at most 64 MiB of HBM per device.

v0:
```python
import jax
import jax.numpy as jnp
from jax import lax
from jax.sharding import PartitionSpec as P

LEAF = 1024
RANK = 256
LEVELS = 3
SLOTS = 2


def from_partner(value, axis, apart):
    return lax.ppermute(value, axis, [(i, i ^ 1 << apart) for i in range(lax.axis_size(axis))])


def passed_along(value, axis, by):
    peers = lax.axis_size(axis)
    pairs = [(i, i + by) for i in range(peers) if 0 <= i + by < peers]
    return lax.ppermute(value, axis, pairs)


def kernel_block(first_points, second_points):
    squared = (first_points[0][:, None] - second_points[0][None, :]) ** 2
    squared = squared + (first_points[1][:, None] - second_points[1][None, :]) ** 2
    squared = squared + (first_points[2][:, None] - second_points[2][None, :]) ** 2
    return jnp.exp(-8.0 * squared)


def upper_bit(device, bit_index):
    return device // 2**bit_index % 2 == 1


def halve_upward(partial_value, tree_level, device):
    for bit_index in range(tree_level - 1, -1, -1):
        half_rows = partial_value.shape[0] // 2
        upper_half = upper_bit(device, bit_index)
        kept_half = jnp.where(upper_half, partial_value[half_rows:], partial_value[:half_rows])
        sent_half = jnp.where(upper_half, partial_value[:half_rows], partial_value[half_rows:])
        partial_value = kept_half + from_partner(sent_half, "leaf", bit_index)
    return partial_value


def group_total(partial_value, tree_level):
    for bit_index in range(tree_level):
        partial_value = partial_value + from_partner(partial_value, "leaf", bit_index)
    return partial_value


def per_device(values, coords, permutation, basis, transfers, couplings, interactions):
    highest = lax.Precision.HIGHEST
    device = lax.axis_index("leaf")
    local_index = permutation % LEAF
    tree_values = jnp.take(values, local_index, axis=0)
    leaf_coeff = jnp.einsum("pr,pc->rc", basis, tree_values, precision=highest)
    blocks = [leaf_coeff]
    offsets = []
    offset = 0
    for tree_level in range(1, LEVELS + 1):
        row_count = RANK // 2 ** (tree_level - 1)
        offsets.append(offset)
        transfer_rows = transfers[offset : offset + row_count]
        offset += row_count
        partial_value = jnp.einsum("qs,qc->sc", transfer_rows, blocks[-1], precision=highest)
        blocks.append(halve_upward(partial_value, tree_level, device))
    local_parts = []
    start = 0
    for tree_level in range(LEVELS + 1):
        stride = 2**tree_level
        row_count = RANK // stride
        own_node = device // stride
        received = []
        for distance in (2, 3, -2, -3):
            received.append(passed_along(blocks[tree_level], "leaf", distance * stride))
        total = jnp.zeros((RANK, blocks[0].shape[1]), jnp.float32)
        for slot_index in range(SLOTS):
            node_delta = interactions[0, tree_level, slot_index] - own_node
            picked = jnp.zeros_like(blocks[tree_level])
            for position, distance in enumerate((2, 3, -2, -3)):
                picked = picked + jnp.where(node_delta == -distance, received[position], 0.0)
            coupling_rows = couplings[start : start + row_count]
            start += row_count
            total = total + jnp.einsum("qr,qc->rc", coupling_rows, picked, precision=highest)
        local_parts.append(total * 2.0 ** (-tree_level / 2.0))
    downward = group_total(local_parts[LEVELS], LEVELS)
    for tree_level in range(LEVELS, 0, -1):
        lower = tree_level - 1
        row_count = RANK // 2**lower
        transfer_rows = transfers[offsets[tree_level - 1] : offsets[tree_level - 1] + row_count]
        parent_term = jnp.dot(transfer_rows, downward, precision=highest)
        row_start = device % 2**lower * row_count
        placed = lax.dynamic_update_slice(jnp.zeros_like(downward), parent_term, (row_start, 0))
        downward = group_total(local_parts[lower] + placed, lower)
    far_tree = jnp.dot(basis, downward, precision=highest)
    far_field = jnp.zeros_like(values).at[local_index].set(far_tree)
    width = values.shape[1]
    packed = jnp.concatenate([values, coords.reshape(3 * LEAF // width, width)], axis=0)
    near_field = jnp.dot(kernel_block(coords, coords), values, precision=highest)
    for distance in (1, -1):
        arrived = passed_along(packed, "leaf", distance)
        near_values = arrived[:LEAF]
        near_points = arrived[LEAF:].reshape(3, LEAF)
        near_field = near_field + jnp.dot(
            kernel_block(coords, near_points), near_values, precision=highest
        )
    return near_field + far_field


def solution(mesh):
    in_specs = (
        P("leaf", None),
        P(None, "leaf"),
        P("leaf"),
        P("leaf", None),
        P("leaf", None),
        P("leaf", None),
        P("leaf", None, None),
    )
    out_specs = P("leaf", None)
    return jax.shard_map(
        per_device, mesh=mesh, in_specs=in_specs, out_specs=out_specs, check_vma=False
    )
```

profile of v0, /device:TPU:24, one launch (start us, length us, event | category | flops | bytes accessed | tf_op | source)
XLA Modules:
  0.0 200.6 jit_solution(6237073063509715174)
XLA Ops:
  1.4 3.8 %gather_fusion = f32[1024,128]{1,0:T(8,128)S(1)} fusion(f32[1024,128]{1,0:T(8,128)} %param.7, s32[1024]{0:T(1024)S(1)} %broadcast_clamp_fusion), kind=kCustom, calls=%fused_computation | custom fusion | bytes 1052672 | tf_op jit(solution)/shard_map/jit(_take)/gather | solution.py:53
  7.2 3.9 %collective-permute-start.2 = (f32[256,128]{0,1:T(8,128)}, f32[256,128]{0,1:T(8,128)S(1)}, u32[]{:S(2)}, u32[]{:S(2)}) collective-permute-start(f32[256,128]{0,1:T(8,128)} %bitcast.10), channel_id=1, source_target_pairs={{0,2},{1,3},{2,4},{3,5},{4,6},{5,7},{6,8},{7,9},{8,10},{9,11},{10,... | collective-permute-start | bytes 393224 | tf_op jit(solution)/shard_map/ppermute | solution.py:19
  11.1 3.0 %collective-permute-start.3 = (f32[256,128]{0,1:T(8,128)}, f32[256,128]{0,1:T(8,128)S(1)}, u32[]{:S(2)}, u32[]{:S(2)}) collective-permute-start(f32[256,128]{0,1:T(8,128)} %bitcast.10), channel_id=1, source_target_pairs={{0,3},{1,4},{2,5},{3,6},{4,7},{5,8},{6,9},{7,10},{8,11},{9,12},{10... | collective-permute-start | bytes 393224 | tf_op jit(solution)/shard_map/ppermute | solution.py:19
  14.1 10.8 %collective-permute-start.4 = (f32[256,128]{0,1:T(8,128)}, f32[256,128]{0,1:T(8,128)S(1)}, u32[]{:S(2)}, u32[]{:S(2)}) collective-permute-start(f32[256,128]{0,1:T(8,128)} %bitcast.10), channel_id=1, source_target_pairs={{2,0},{3,1},{4,2},{5,3},{6,4},{7,5},{8,6},{9,7},{10,8},{11,9},{12,... | collective-permute-start | bytes 393224 | tf_op jit(solution)/shard_map/ppermute | solution.py:19
  24.9 4.3 %collective-permute-start.5 = (f32[256,128]{0,1:T(8,128)}, f32[256,128]{0,1:T(8,128)}, u32[]{:S(2)}, u32[]{:S(2)}) collective-permute-start(f32[256,128]{0,1:T(8,128)} %bitcast.10), channel_id=1, source_target_pairs={{3,0},{4,1},{5,2},{6,3},{7,4},{8,5},{9,6},{10,7},{11,8},{12,9},{13... | collective-permute-start | bytes 393224 | tf_op jit(solution)/shard_map/ppermute | solution.py:19
  33.9 1.9 collective-permute-start.11
  35.9 5.4 %fusion.22 = f32[1024,128]{1,0:T(8,128)} fusion(f32[1024,128]{1,0:T(8,128)S(1)} %copy-done.1, f32[1024]{0:T(1024)S(1)} %bitcast.55, f32[1024]{0:T(1024)S(1)} %bitcast.52, f32[1024]{0:T(1024)S(1)} %bitcast.49), kind=kOutput, calls=%fused_computation.24 | convolution fusion | flops 1620049920 | bytes 1060864 | tf_op jit(solution)/shard_map/dot_general | solution.py:97
  42.0 2.1 %collective-permute-start.12 = (f32[64,128]{0,1:T(8,128)}, f32[64,128]{0,1:T(8,128)}, u32[]{:S(2)}, u32[]{:S(2)}) collective-permute-start(f32[64,128]{0,1:T(8,128)} %slice_select_fusion.3), channel_id=1, source_target_pairs={{0,1},{1,0},{2,3},{3,2},{4,5},{5,4},{6,7},{7,6},{8,9},{9,8},{10,11... | collective-permute-start | bytes 98312 | tf_op jit(solution)/shard_map/ppermute | solution.py:13
  48.2 1.9 collective-permute-start.17
  50.8 4.5 %collective-permute-done.17 = f32[128,128]{0,1:T(8,128)S(1)} collective-permute-done((f32[128,128]{0,1:T(8,128)S(1)}, f32[128,128]{0,1:T(8,128)S(1)}, u32[]{:S(2)}, u32[]{:S(2)}) %collective-permute-start.17) | collective-permute-done | bytes 65568 | tf_op jit(solution)/shard_map/ppermute | solution.py:13
  55.3 3.9 %collective-permute-start.18 = (f32[64,128]{0,1:T(8,128)S(1)}, f32[64,128]{0,1:T(8,128)S(1)}, u32[]{:S(2)}, u32[]{:S(2)}) collective-permute-start(f32[64,128]{0,1:T(8,128)S(1)} %slice_select_fusion.1), channel_id=1, source_target_pairs={{0,2},{1,3},{2,0},{3,1},{4,6},{5,7},{6,4},{7,5},{8,10},{9,11},{10,... | collective-permute-start | bytes 98312 | tf_op jit(solution)/shard_map/ppermute | solution.py:13
  64.9 7.3 %collective-permute-start.10 = (f32[128,128]{0,1:T(8,128)S(1)}, f32[128,128]{0,1:T(8,128)S(1)}, u32[]{:S(2)}, u32[]{:S(2)}) collective-permute-start(f32[128,128]{0,1:T(8,128)S(1)} %select_add_fusion.5), channel_id=1, source_target_pairs={{6,0},{7,1},{8,2},{9,3},{10,4},{11,5},{12,6},{13,7},{14,8},{15,9},... | collective-permute-start | bytes 196616 | tf_op jit(solution)/shard_map/ppermute | solution.py:19
  72.4 1.9 collective-permute-start.7
  74.3 2.6 %collective-permute-start.8 = (f32[128,128]{0,1:T(8,128)S(1)}, f32[128,128]{0,1:T(8,128)S(1)}, u32[]{:S(2)}, u32[]{:S(2)}) collective-permute-start(f32[128,128]{0,1:T(8,128)S(1)} %select_add_fusion.5), channel_id=1, source_target_pairs={{0,6},{1,7},{2,8},{3,9},{4,10},{5,11},{6,12},{7,13},{8,14},{9,15},... | collective-permute-start | bytes 196616 | tf_op jit(solution)/shard_map/ppermute | solution.py:19
  76.9 8.4 %collective-permute-start.9 = (f32[128,128]{0,1:T(8,128)S(1)}, f32[128,128]{0,1:T(8,128)S(1)}, u32[]{:S(2)}, u32[]{:S(2)}) collective-permute-start(f32[128,128]{0,1:T(8,128)S(1)} %select_add_fusion.5), channel_id=1, source_target_pairs={{4,0},{5,1},{6,2},{7,3},{8,4},{9,5},{10,6},{11,7},{12,8},{13,9},{1... | collective-permute-start | bytes 196616 | tf_op jit(solution)/shard_map/ppermute | solution.py:19
  88.6 2.8 %collective-permute-start.20 = (f32[32,128]{0,1:T(8,128)S(1)}, f32[32,128]{0,1:T(8,128)S(1)}, u32[]{:S(2)}, u32[]{:S(2)}) collective-permute-start(f32[32,128]{0,1:T(8,128)S(1)} %select_add_fusion), channel_id=1, source_target_pairs={{0,16},{1,17},{2,18},{3,19},{4,20},{5,21},{6,22},{7,23},{8,24},{9,... | collective-permute-start | bytes 49160 | tf_op jit(solution)/shard_map/ppermute | solution.py:19
  91.4 3.4 %collective-permute-start.21 = (f32[32,128]{0,1:T(8,128)S(1)}, f32[32,128]{0,1:T(8,128)S(1)}, u32[]{:S(2)}, u32[]{:S(2)}) collective-permute-start(f32[32,128]{0,1:T(8,128)S(1)} %select_add_fusion), channel_id=1, source_target_pairs={{0,24},{1,25},{2,26},{3,27},{4,28},{5,29},{6,30},{7,31},{8,32},{9,... | collective-permute-start | bytes 49160 | tf_op jit(solution)/shard_map/ppermute | solution.py:19
  94.8 13.3 %collective-permute-start.22 = (f32[32,128]{0,1:T(8,128)S(1)}, f32[32,128]{0,1:T(8,128)S(1)}, u32[]{:S(2)}, u32[]{:S(2)}) collective-permute-start(f32[32,128]{0,1:T(8,128)S(1)} %select_add_fusion), channel_id=1, source_target_pairs={{16,0},{17,1},{18,2},{19,3},{20,4},{21,5},{22,6},{23,7},{24,8},{25... | collective-permute-start | bytes 49160 | tf_op jit(solution)/shard_map/ppermute | solution.py:19
  108.1 8.7 %collective-permute-start.23 = (f32[32,128]{0,1:T(8,128)S(1)}, f32[32,128]{0,1:T(8,128)S(1)}, u32[]{:S(2)}, u32[]{:S(2)}) collective-permute-start(f32[32,128]{0,1:T(8,128)S(1)} %select_add_fusion), channel_id=1, source_target_pairs={{24,0},{25,1},{26,2},{27,3},{28,4},{29,5},{30,6},{31,7},{32,8},{33... | collective-permute-start | bytes 49160 | tf_op jit(solution)/shard_map/ppermute | solution.py:19
  119.1 3.8 %collective-permute-start.14 = (f32[64,128]{0,1:T(8,128)}, f32[64,128]{0,1:T(8,128)S(1)}, u32[]{:S(2)}, u32[]{:S(2)}) collective-permute-start(f32[64,128]{0,1:T(8,128)} %select_add_fusion.3), channel_id=1, source_target_pairs={{0,12},{1,13},{2,14},{3,15},{4,16},{5,17},{6,18},{7,19},{8,20},{9,... | collective-permute-start | bytes 98312 | tf_op jit(solution)/shard_map/ppermute | solution.py:19
  122.8 9.0 %collective-permute-start.15 = (f32[64,128]{0,1:T(8,128)}, f32[64,128]{0,1:T(8,128)S(1)}, u32[]{:S(2)}, u32[]{:S(2)}) collective-permute-start(f32[64,128]{0,1:T(8,128)} %select_add_fusion.3), channel_id=1, source_target_pairs={{8,0},{9,1},{10,2},{11,3},{12,4},{13,5},{14,6},{15,7},{16,8},{17,9... | collective-permute-start | bytes 98312 | tf_op jit(solution)/shard_map/ppermute | solution.py:19
  131.8 10.8 %collective-permute-start.16 = (f32[64,128]{0,1:T(8,128)}, f32[64,128]{0,1:T(8,128)S(1)}, u32[]{:S(2)}, u32[]{:S(2)}) collective-permute-start(f32[64,128]{0,1:T(8,128)} %select_add_fusion.3), channel_id=1, source_target_pairs={{12,0},{13,1},{14,2},{15,3},{16,4},{17,5},{18,6},{19,7},{20,8},{21... | collective-permute-start | bytes 98312 | tf_op jit(solution)/shard_map/ppermute | solution.py:19
  148.4 2.4 %collective-permute-start = (f32[1048,128]{1,0:T(8,128)}, f32[1048,128]{1,0:T(8,128)}, u32[]{:S(2)}, u32[]{:S(2)}) collective-permute-start(f32[1048,128]{1,0:T(8,128)} %constant_dynamic-update-slice_fusion), channel_id=1, source_target_pairs={{0,1},{1,2},{2,3},{3,4},{4,5},{5,6},{6,7},{7,8},{8,9},{9,10},{10,1... | collective-permute-start | bytes 1609736 | tf_op jit(solution)/shard_map/ppermute | solution.py:19
  150.9 3.2 %collective-permute-start.25 = (f32[256,128]{0,1:T(8,128)S(1)}, f32[256,128]{0,1:T(8,128)S(1)}, u32[]{:S(2)}, u32[]{:S(2)}) collective-permute-start(f32[256,128]{0,1:T(8,128)S(1)} %add.258), channel_id=1, source_target_pairs={{0,2},{1,3},{2,0},{3,1},{4,6},{5,7},{6,4},{7,5},{8,10},{9,11},{10,... | collective-permute-start | bytes 393224 | tf_op jit(solution)/shard_map/ppermute | solution.py:13
  154.3 6.1 %collective-permute-done.25 = f32[256,128]{0,1:T(8,128)S(1)} collective-permute-done((f32[256,128]{0,1:T(8,128)S(1)}, f32[256,128]{0,1:T(8,128)S(1)}, u32[]{:S(2)}, u32[]{:S(2)}) %collective-permute-start.25) | collective-permute-done | bytes 131104 | tf_op jit(solution)/shard_map/ppermute | solution.py:13
  162.7 9.2 %collective-permute-done.26 = f32[256,128]{0,1:T(8,128)S(1)} collective-permute-done((f32[256,128]{0,1:T(8,128)S(1)}, f32[256,128]{0,1:T(8,128)S(1)}, u32[]{:S(2)}, u32[]{:S(2)}) %collective-permute-start.26) | collective-permute-done | bytes 131104 | tf_op jit(solution)/shard_map/ppermute | solution.py:13
  172.8 2.2 %collective-permute-start.27 = (f32[256,128]{0,1:T(8,128)S(1)}, f32[256,128]{0,1:T(8,128)S(1)}, u32[]{:S(2)}, u32[]{:S(2)}) collective-permute-start(f32[256,128]{0,1:T(8,128)S(1)} %add.261), channel_id=1, source_target_pairs={{0,1},{1,0},{2,3},{3,2},{4,5},{5,4},{6,7},{7,6},{8,9},{9,8},{10,11... | collective-permute-start | bytes 393224 | tf_op jit(solution)/shard_map/ppermute | solution.py:13
  176.1 2.1 %collective-permute-start.28 = (f32[256,128]{0,1:T(8,128)S(1)}, f32[256,128]{0,1:T(8,128)S(1)}, u32[]{:S(2)}, u32[]{:S(2)}) collective-permute-start(f32[256,128]{0,1:T(8,128)S(1)} %add.262), channel_id=1, source_target_pairs={{0,2},{1,3},{2,0},{3,1},{4,6},{5,7},{6,4},{7,5},{8,10},{9,11},{10,... | collective-permute-start | bytes 393224 | tf_op jit(solution)/shard_map/ppermute | solution.py:13
  178.2 6.5 %fusion = f32[1024,128]{1,0:T(8,128)} fusion(f32[1024]{0:T(1024)S(1)} %get-tuple-element.11, f32[1024]{0:T(1024)S(1)} %get-tuple-element.12, f32[1024]{0:T(1024)S(1)} %get-tuple-element.10, f32[1024]{0:T(1024)S(1)} %bitcast.56, f32[1024]{0:T(1024)S(1)} %bitcast.53, f32[1024]{0:T(1024)S(1)} %bitcast.50, f32[1048,128]{1,0:T(8,128)} %collective-permute-done.1), kind=kOutput, calls=%fused_computation.2 | convolution fusion | flops 1620049920 | bytes 1073152 | tf_op jit(solution)/shard_map/dot_general | solution.py:102
  185.0 2.2 %collective-permute-start.29 = (f32[256,128]{0,1:T(8,128)S(1)}, f32[256,128]{0,1:T(8,128)S(1)}, u32[]{:S(2)}, u32[]{:S(2)}) collective-permute-start(f32[256,128]{0,1:T(8,128)S(1)} %bitcast_dynamic-update-slice_fusion), channel_id=1, source_target_pairs={{0,1},{1,0},{2,3},{3,2},{4,5},{5,4},{6,7},{7,6},{8,9},{9,8},{10,11... | collective-permute-start | bytes 393224 | tf_op jit(solution)/shard_map/ppermute | solution.py:13
  190.4 3.6 %scatter_custom_fusion = f32[1024,128]{1,0:T(8,128)S(1)} fusion(s32[1024]{0:T(1024)} %copy-done.6, f32[1024,128]{1,0:T(8,128)S(1)} %copy.9, f32[]{:T(128)} %constant.133.clone.1), kind=kCustom, calls=%fused_computation.80 | custom fusion | bytes 524800 | tf_op jit(solution)/shard_map/scatter | solution.py:94
  194.0 6.7 %fusion.60 = f32[1024,128]{1,0:T(8,128)} fusion(f32[1024,128]{1,0:T(8,128)S(1)} %scatter_custom_fusion, f32[1024,128]{1,0:T(8,128)} %fusion, f32[1024,128]{1,0:T(8,128)S(1)} %copy-done.8, f32[1024]{0:T(1024)S(1)} %get-tuple-element.8, f32[1024]{0:T(1024)S(1)} %get-tuple-element.9, f32[1024]{0:T(1024)S(1)} %get-tuple-element.7, f32[1024]{0:T(1024)S(1)} %bitcast.57, ...), kind=kOutput, calls=%fused_computation.59 | convolution fusion | flops 1620443136 | bytes 2646016 | tf_op jit(solution)/shard_map/dot_general | solution.py:102
  (94 shorter events, 33.1 us)
Async XLA Ops:
  7.1 28.7 %copy-start.1 = (f32[1024,128]{1,0:T(8,128)S(1)}, f32[1024,128]{1,0:T(8,128)}, u32[]{:S(2)}) copy-start(f32[1024,128]{1,0:T(8,128)} %param.7) | copy-start | bytes 1572868
  7.2 65.2 %collective-permute-start.2 = (f32[256,128]{0,1:T(8,128)}, f32[256,128]{0,1:T(8,128)S(1)}, u32[]{:S(2)}, u32[]{:S(2)}) collective-permute-start(f32[256,128]{0,1:T(8,128)} %bitcast.10), channel_id=1, source_target_pairs={{0,2},{1,3},{2,4},{3,5},{4,6},{5,7},{6,8},{7,9},{8,10},{9,11},{10,... | collective-permute-start | bytes 393224 | tf_op jit(solution)/shard_map/ppermute | solution.py:19
  11.1 63.2 %collective-permute-start.3 = (f32[256,128]{0,1:T(8,128)}, f32[256,128]{0,1:T(8,128)S(1)}, u32[]{:S(2)}, u32[]{:S(2)}) collective-permute-start(f32[256,128]{0,1:T(8,128)} %bitcast.10), channel_id=1, source_target_pairs={{0,3},{1,4},{2,5},{3,6},{4,7},{5,8},{6,9},{7,10},{8,11},{9,12},{10... | collective-permute-start | bytes 393224 | tf_op jit(solution)/shard_map/ppermute | solution.py:19
  14.1 62.8 %collective-permute-start.4 = (f32[256,128]{0,1:T(8,128)}, f32[256,128]{0,1:T(8,128)S(1)}, u32[]{:S(2)}, u32[]{:S(2)}) collective-permute-start(f32[256,128]{0,1:T(8,128)} %bitcast.10), channel_id=1, source_target_pairs={{2,0},{3,1},{4,2},{5,3},{6,4},{7,5},{8,6},{9,7},{10,8},{11,9},{12,... | collective-permute-start | bytes 393224 | tf_op jit(solution)/shard_map/ppermute | solution.py:19
  24.9 60.4 %collective-permute-start.5 = (f32[256,128]{0,1:T(8,128)}, f32[256,128]{0,1:T(8,128)}, u32[]{:S(2)}, u32[]{:S(2)}) collective-permute-start(f32[256,128]{0,1:T(8,128)} %bitcast.10), channel_id=1, source_target_pairs={{3,0},{4,1},{5,2},{6,3},{7,4},{8,5},{9,6},{10,7},{11,8},{12,9},{13... | collective-permute-start | bytes 393224 | tf_op jit(solution)/shard_map/ppermute | solution.py:19
  30.5 3.1 %collective-permute-start.6 = (f32[128,128]{0,1:T(8,128)S(1)}, f32[128,128]{0,1:T(8,128)S(1)}, u32[]{:S(2)}, u32[]{:S(2)}) collective-permute-start(f32[128,128]{0,1:T(8,128)S(1)} %slice_select_fusion.5), channel_id=1, source_target_pairs={{0,1},{1,0},{2,3},{3,2},{4,5},{5,4},{6,7},{7,6},{8,9},{9,8},{10,11... | collective-permute-start | bytes 196616 | tf_op jit(solution)/shard_map/ppermute | solution.py:13
  33.9 7.4 %collective-permute-start.11 = (f32[128,128]{0,1:T(8,128)S(1)}, f32[128,128]{0,1:T(8,128)S(1)}, u32[]{:S(2)}, u32[]{:S(2)}) collective-permute-start(f32[128,128]{0,1:T(8,128)S(1)} %slice_select_fusion.4), channel_id=1, source_target_pairs={{0,2},{1,3},{2,0},{3,1},{4,6},{5,7},{6,4},{7,5},{8,10},{9,11},{10,... | collective-permute-start | bytes 196616 | tf_op jit(solution)/shard_map/ppermute | solution.py:13
  42.0 3.5 %collective-permute-start.12 = (f32[64,128]{0,1:T(8,128)}, f32[64,128]{0,1:T(8,128)}, u32[]{:S(2)}, u32[]{:S(2)}) collective-permute-start(f32[64,128]{0,1:T(8,128)} %slice_select_fusion.3), channel_id=1, source_target_pairs={{0,1},{1,0},{2,3},{3,2},{4,5},{5,4},{6,7},{7,6},{8,9},{9,8},{10,11... | collective-permute-start | bytes 98312 | tf_op jit(solution)/shard_map/ppermute | solution.py:13
  44.9 42.3 %copy-start.3 = (f32[960,256]{1,0:T(8,128)S(1)}, f32[960,256]{1,0:T(8,128)}, u32[]{:S(2)}) copy-start(f32[960,256]{1,0:T(8,128)} %param.12) | copy-start | bytes 2949124
  48.2 7.1 %collective-permute-start.17 = (f32[128,128]{0,1:T(8,128)S(1)}, f32[128,128]{0,1:T(8,128)S(1)}, u32[]{:S(2)}, u32[]{:S(2)}) collective-permute-start(f32[128,128]{0,1:T(8,128)S(1)} %slice_select_fusion.2), channel_id=1, source_target_pairs={{0,4},{1,5},{2,6},{3,7},{4,0},{5,1},{6,2},{7,3},{8,12},{9,13},{10,... | collective-permute-start | bytes 196616 | tf_op jit(solution)/shard_map/ppermute | solution.py:13
  55.3 9.5 %collective-permute-start.18 = (f32[64,128]{0,1:T(8,128)S(1)}, f32[64,128]{0,1:T(8,128)S(1)}, u32[]{:S(2)}, u32[]{:S(2)}) collective-permute-start(f32[64,128]{0,1:T(8,128)S(1)} %slice_select_fusion.1), channel_id=1, source_target_pairs={{0,2},{1,3},{2,0},{3,1},{4,6},{5,7},{6,4},{7,5},{8,10},{9,11},{10,... | collective-permute-start | bytes 98312 | tf_op jit(solution)/shard_map/ppermute | solution.py:13
  64.9 26.5 %collective-permute-start.10 = (f32[128,128]{0,1:T(8,128)S(1)}, f32[128,128]{0,1:T(8,128)S(1)}, u32[]{:S(2)}, u32[]{:S(2)}) collective-permute-start(f32[128,128]{0,1:T(8,128)S(1)} %select_add_fusion.5), channel_id=1, source_target_pairs={{6,0},{7,1},{8,2},{9,3},{10,4},{11,5},{12,6},{13,7},{14,8},{15,9},... | collective-permute-start | bytes 196616 | tf_op jit(solution)/shard_map/ppermute | solution.py:19
  72.4 22.4 %collective-permute-start.7 = (f32[128,128]{0,1:T(8,128)S(1)}, f32[128,128]{0,1:T(8,128)S(1)}, u32[]{:S(2)}, u32[]{:S(2)}) collective-permute-start(f32[128,128]{0,1:T(8,128)S(1)} %select_add_fusion.5), channel_id=1, source_target_pairs={{0,4},{1,5},{2,6},{3,7},{4,8},{5,9},{6,10},{7,11},{8,12},{9,13},{1... | collective-permute-start | bytes 196616 | tf_op jit(solution)/shard_map/ppermute | solution.py:19
  74.3 33.8 %collective-permute-start.8 = (f32[128,128]{0,1:T(8,128)S(1)}, f32[128,128]{0,1:T(8,128)S(1)}, u32[]{:S(2)}, u32[]{:S(2)}) collective-permute-start(f32[128,128]{0,1:T(8,128)S(1)} %select_add_fusion.5), channel_id=1, source_target_pairs={{0,6},{1,7},{2,8},{3,9},{4,10},{5,11},{6,12},{7,13},{8,14},{9,15},... | collective-permute-start | bytes 196616 | tf_op jit(solution)/shard_map/ppermute | solution.py:19
  76.9 39.9 %collective-permute-start.9 = (f32[128,128]{0,1:T(8,128)S(1)}, f32[128,128]{0,1:T(8,128)S(1)}, u32[]{:S(2)}, u32[]{:S(2)}) collective-permute-start(f32[128,128]{0,1:T(8,128)S(1)} %select_add_fusion.5), channel_id=1, source_target_pairs={{4,0},{5,1},{6,2},{7,3},{8,4},{9,5},{10,6},{11,7},{12,8},{13,9},{1... | collective-permute-start | bytes 196616 | tf_op jit(solution)/shard_map/ppermute | solution.py:19
  85.3 3.2 %collective-permute-start.19 = (f32[32,128]{0,1:T(8,128)S(1)}, f32[32,128]{0,1:T(8,128)S(1)}, u32[]{:S(2)}, u32[]{:S(2)}) collective-permute-start(f32[32,128]{0,1:T(8,128)S(1)} %slice_select_fusion), channel_id=1, source_target_pairs={{0,1},{1,0},{2,3},{3,2},{4,5},{5,4},{6,7},{7,6},{8,9},{9,8},{10,11... | collective-permute-start | bytes 49160 | tf_op jit(solution)/shard_map/ppermute | solution.py:13
  88.6 30.5 %collective-permute-start.20 = (f32[32,128]{0,1:T(8,128)S(1)}, f32[32,128]{0,1:T(8,128)S(1)}, u32[]{:S(2)}, u32[]{:S(2)}) collective-permute-start(f32[32,128]{0,1:T(8,128)S(1)} %select_add_fusion), channel_id=1, source_target_pairs={{0,16},{1,17},{2,18},{3,19},{4,20},{5,21},{6,22},{7,23},{8,24},{9,... | collective-permute-start | bytes 49160 | tf_op jit(solution)/shard_map/ppermute | solution.py:19
  91.4 31.5 %collective-permute-start.21 = (f32[32,128]{0,1:T(8,128)S(1)}, f32[32,128]{0,1:T(8,128)S(1)}, u32[]{:S(2)}, u32[]{:S(2)}) collective-permute-start(f32[32,128]{0,1:T(8,128)S(1)} %select_add_fusion), channel_id=1, source_target_pairs={{0,24},{1,25},{2,26},{3,27},{4,28},{5,29},{6,30},{7,31},{8,32},{9,... | collective-permute-start | bytes 49160 | tf_op jit(solution)/shard_map/ppermute | solution.py:19
  94.8 37.0 %collective-permute-start.22 = (f32[32,128]{0,1:T(8,128)S(1)}, f32[32,128]{0,1:T(8,128)S(1)}, u32[]{:S(2)}, u32[]{:S(2)}) collective-permute-start(f32[32,128]{0,1:T(8,128)S(1)} %select_add_fusion), channel_id=1, source_target_pairs={{16,0},{17,1},{18,2},{19,3},{20,4},{21,5},{22,6},{23,7},{24,8},{25... | collective-permute-start | bytes 49160 | tf_op jit(solution)/shard_map/ppermute | solution.py:19
  108.1 34.6 %collective-permute-start.23 = (f32[32,128]{0,1:T(8,128)S(1)}, f32[32,128]{0,1:T(8,128)S(1)}, u32[]{:S(2)}, u32[]{:S(2)}) collective-permute-start(f32[32,128]{0,1:T(8,128)S(1)} %select_add_fusion), channel_id=1, source_target_pairs={{24,0},{25,1},{26,2},{27,3},{28,4},{29,5},{30,6},{31,7},{32,8},{33... | collective-permute-start | bytes 49160 | tf_op jit(solution)/shard_map/ppermute | solution.py:19
  117.1 31.3 %collective-permute-start.13 = (f32[64,128]{0,1:T(8,128)}, f32[64,128]{0,1:T(8,128)S(1)}, u32[]{:S(2)}, u32[]{:S(2)}) collective-permute-start(f32[64,128]{0,1:T(8,128)} %select_add_fusion.3), channel_id=1, source_target_pairs={{0,8},{1,9},{2,10},{3,11},{4,12},{5,13},{6,14},{7,15},{8,16},{9,17... | collective-permute-start | bytes 98312 | tf_op jit(solution)/shard_map/ppermute | solution.py:19
  119.1 31.8 %collective-permute-start.14 = (f32[64,128]{0,1:T(8,128)}, f32[64,128]{0,1:T(8,128)S(1)}, u32[]{:S(2)}, u32[]{:S(2)}) collective-permute-start(f32[64,128]{0,1:T(8,128)} %select_add_fusion.3), channel_id=1, source_target_pairs={{0,12},{1,13},{2,14},{3,15},{4,16},{5,17},{6,18},{7,19},{8,20},{9,... | collective-permute-start | bytes 98312 | tf_op jit(solution)/shard_map/ppermute | solution.py:19
  122.8 31.2 %collective-permute-start.15 = (f32[64,128]{0,1:T(8,128)}, f32[64,128]{0,1:T(8,128)S(1)}, u32[]{:S(2)}, u32[]{:S(2)}) collective-permute-start(f32[64,128]{0,1:T(8,128)} %select_add_fusion.3), channel_id=1, source_target_pairs={{8,0},{9,1},{10,2},{11,3},{12,4},{13,5},{14,6},{15,7},{16,8},{17,9... | collective-permute-start | bytes 98312 | tf_op jit(solution)/shard_map/ppermute | solution.py:19
  131.8 22.2 %collective-permute-start.16 = (f32[64,128]{0,1:T(8,128)}, f32[64,128]{0,1:T(8,128)S(1)}, u32[]{:S(2)}, u32[]{:S(2)}) collective-permute-start(f32[64,128]{0,1:T(8,128)} %select_add_fusion.3), channel_id=1, source_target_pairs={{12,0},{13,1},{14,2},{15,3},{16,4},{17,5},{18,6},{19,7},{20,8},{21... | collective-permute-start | bytes 98312 | tf_op jit(solution)/shard_map/ppermute | solution.py:19
  143.2 3.2 %collective-permute-start.24 = (f32[256,128]{0,1:T(8,128)S(1)}, f32[256,128]{0,1:T(8,128)S(1)}, u32[]{:S(2)}, u32[]{:S(2)}) collective-permute-start(f32[256,128]{0,1:T(8,128)S(1)} %fusion.67), channel_id=1, source_target_pairs={{0,1},{1,0},{2,3},{3,2},{4,5},{5,4},{6,7},{7,6},{8,9},{9,8},{10,11... | collective-permute-start | bytes 393224 | tf_op jit(solution)/shard_map/ppermute | solution.py:13
  146.5 28.6 %collective-permute-start.1 = (f32[1048,128]{1,0:T(8,128)}, f32[1048,128]{1,0:T(8,128)}, u32[]{:S(2)}, u32[]{:S(2)}) collective-permute-start(f32[1048,128]{1,0:T(8,128)} %constant_dynamic-update-slice_fusion), channel_id=1, source_target_pairs={{1,0},{2,1},{3,2},{4,3},{5,4},{6,5},{7,6},{8,7},{9,8},{10,9},{11,1... | collective-permute-start | bytes 1609736 | tf_op jit(solution)/shard_map/ppermute | solution.py:19
  148.4 38.8 %collective-permute-start = (f32[1048,128]{1,0:T(8,128)}, f32[1048,128]{1,0:T(8,128)}, u32[]{:S(2)}, u32[]{:S(2)}) collective-permute-start(f32[1048,128]{1,0:T(8,128)} %constant_dynamic-update-slice_fusion), channel_id=1, source_target_pairs={{0,1},{1,2},{2,3},{3,4},{4,5},{5,6},{6,7},{7,8},{8,9},{9,10},{10,1... | collective-permute-start | bytes 1609736 | tf_op jit(solution)/shard_map/ppermute | solution.py:19
  150.9 9.6 %collective-permute-start.25 = (f32[256,128]{0,1:T(8,128)S(1)}, f32[256,128]{0,1:T(8,128)S(1)}, u32[]{:S(2)}, u32[]{:S(2)}) collective-permute-start(f32[256,128]{0,1:T(8,128)S(1)} %add.258), channel_id=1, source_target_pairs={{0,2},{1,3},{2,0},{3,1},{4,6},{5,7},{6,4},{7,5},{8,10},{9,11},{10,... | collective-permute-start | bytes 393224 | tf_op jit(solution)/shard_map/ppermute | solution.py:13
  160.5 11.4 %collective-permute-start.26 = (f32[256,128]{0,1:T(8,128)S(1)}, f32[256,128]{0,1:T(8,128)S(1)}, u32[]{:S(2)}, u32[]{:S(2)}) collective-permute-start(f32[256,128]{0,1:T(8,128)S(1)} %add.259), channel_id=1, source_target_pairs={{0,4},{1,5},{2,6},{3,7},{4,0},{5,1},{6,2},{7,3},{8,12},{9,13},{10,... | collective-permute-start | bytes 393224 | tf_op jit(solution)/shard_map/ppermute | solution.py:13
  172.8 3.2 %collective-permute-start.27 = (f32[256,128]{0,1:T(8,128)S(1)}, f32[256,128]{0,1:T(8,128)S(1)}, u32[]{:S(2)}, u32[]{:S(2)}) collective-permute-start(f32[256,128]{0,1:T(8,128)S(1)} %add.261), channel_id=1, source_target_pairs={{0,1},{1,0},{2,3},{3,2},{4,5},{5,4},{6,7},{7,6},{8,9},{9,8},{10,11... | collective-permute-start | bytes 393224 | tf_op jit(solution)/shard_map/ppermute | solution.py:13
  176.1 8.6 %collective-permute-start.28 = (f32[256,128]{0,1:T(8,128)S(1)}, f32[256,128]{0,1:T(8,128)S(1)}, u32[]{:S(2)}, u32[]{:S(2)}) collective-permute-start(f32[256,128]{0,1:T(8,128)S(1)} %add.262), channel_id=1, source_target_pairs={{0,2},{1,3},{2,0},{3,1},{4,6},{5,7},{6,4},{7,5},{8,10},{9,11},{10,... | collective-permute-start | bytes 393224 | tf_op jit(solution)/shard_map/ppermute | solution.py:13
  185.0 3.2 %collective-permute-start.29 = (f32[256,128]{0,1:T(8,128)S(1)}, f32[256,128]{0,1:T(8,128)S(1)}, u32[]{:S(2)}, u32[]{:S(2)}) collective-permute-start(f32[256,128]{0,1:T(8,128)S(1)} %bitcast_dynamic-update-slice_fusion), channel_id=1, source_target_pairs={{0,1},{1,0},{2,3},{3,2},{4,5},{5,4},{6,7},{7,6},{8,9},{9,8},{10,11... | collective-permute-start | bytes 393224 | tf_op jit(solution)/shard_map/ppermute | solution.py:13
  (7 other events, 76.0 us)
where the time goes:
time: 203 us; the launch traced here: 201 us
  starting transfers between devices  127 us (63%)
  matrix products  28.3 us (14%)
  waiting for transfers between devices  22.6 us (11%)
  local copies, waits for them, and re-layouts  13 us (6%)
  between operations  5.8 us (3%)
  other arithmetic  3.49 us (2%)
    ppermute x18, starting transfers between devices, passed_along(): return lax.ppermute(value, axis, pairs)  100 us
    ppermute x12, starting transfers between devices, from_partner(): lax.ppermute(value, axis, [(i, i ^ 1 << apart) for i in range(lax.axis_si...  27.2 us
    ppermute x12, waiting for transfers between devices, from_partner(): lax.ppermute(value, axis, [(i, i ^ 1 << apart) for i in range(lax.axis_si...  22.5 us
    dot_general x2, matrix products, per_device(): jnp.dot(kernel_block(coords, near_points), near_values, precision=highest)  13.2 us
    dot_general x1, matrix products, per_device(): jnp.dot(kernel_block(coords, coords), values, precision=highest)  5.44 us
  transfers between devices with their start and end apart: 30, of which 8 were waited for; matrix products, arithmetic and copies ran while one was open for 13% of the time, Pallas kernels for 0%

commit v1 on v0

v1 whole, which is shorter than its diff:
```python
import functools
import math

import jax
import jax.numpy as jnp
from jax import lax
from jax.experimental import pallas as pl
from jax.experimental.pallas import tpu as pltpu
from jax.sharding import PartitionSpec as P

LEAF = 1024
RANK = 256
NCOL = 128
N_LEAF = 512
ROWS = 256
MESH = pl.DeviceIdType.MESH
F32 = jnp.float32
BF16 = jnp.bfloat16
NT = (((1,), (1,)), ((), ()))
NN = (((1,), (0,)), ((), ()))
SCALE = math.sqrt(8.0 * math.log2(math.e))


def split(x):
    hi = x.astype(BF16)
    return hi, (x - hi.astype(F32)).astype(BF16)


def dot(a, b, dims=NN):
    return lax.dot_general(a, b, dims, preferred_element_type=F32)


def dot3(a, b, dims=NN):
    a_hi, a_lo = a
    b_hi, b_lo = b
    return dot(a_hi, b_hi, dims) + (dot(a_hi, b_lo, dims) + dot(a_lo, b_hi, dims))


def kernel(
    values, coords, perm, basis, transfers, couplings, inter, out,
    val, bas, e1, e2, e3, cpl, cs, pc, vst, nst, nv, nc, oh_b, bt_hi, bt_lo,
    c0, t1, t1r, c1, t2, t2r, t3, t3r, c2, c3, r0, r1, r2, r3,
    yh, yhr, h2, h2r, h3, h3r, f3, f1, y0,
    loc, snd, rcv,
):
    me = lax.axis_index("leaf")
    core = me % 2
    quarter = me % 4
    eighth = me % 8

    def at(offset):
        return (me + offset + N_LEAF) % N_LEAF

    p1 = me + 1 - 2 * core
    p2 = me + 2 - 4 * (me // 2 % 2)
    p4 = me + 4 - 8 * (me // 4 % 2)
    p6 = p2 + 4 - 8 * (me // 4 % 2)

    local = []

    def bring(src, dst):
        copy = pltpu.make_async_copy(src, dst, loc.at[len(local)])
        copy.start()
        local.append(copy)
        return copy

    e2_row = pl.multiple_of(core * 128, 128)
    e3_row = pl.multiple_of(quarter * 64, 64)
    get_basis = bring(basis, bas)
    get_values = bring(values, val)
    get_e1 = bring(transfers.at[pl.ds(0, 256)], e1)
    get_e2 = bring(transfers.at[pl.ds(256, 128)], e2.at[pl.ds(e2_row, 128)])
    get_e3 = bring(transfers.at[pl.ds(384, 64)], e3.at[pl.ds(e3_row, 64)])
    get_cpl = bring(couplings, cpl)

    barrier = pltpu.get_barrier_semaphore()
    greet = [at(o) for o in (1, -1, 2, -2, 4, -4, 8, -8, 24, -24)] + [p1, p2, p4, p6]
    for peer in greet:
        pl.semaphore_signal(barrier, inc=1, device_id=(peer,), device_id_type=MESH)

    cs[pl.ds(0, 3), :] = coords[...] * SCALE
    cs[pl.ds(3, 5), :] = jnp.zeros((5, LEAF), F32)
    pc[...] = cs[...].T

    pl.semaphore_wait(barrier, len(greet))

    used = []

    def send(src, dst, peer):
        index = len(used)
        copy = pltpu.make_async_remote_copy(
            src_ref=src, dst_ref=dst, send_sem=snd.at[index], recv_sem=rcv.at[index],
            device_id=(peer,), device_id_type=MESH,
        )
        copy.start()
        used.append(copy)
        return copy

    e3_own = e3.at[pl.ds(e3_row, 64)]
    e3_far = send(transfers.at[pl.ds(384, 64)], e3_own, p2)
    e3_near = send(transfers.at[pl.ds(384, 64)], e3_own, p1)
    e2_near = send(transfers.at[pl.ds(256, 128)], e2.at[pl.ds(e2_row, 128)], p1)
    n_up = send(values, nv.at[0], at(1))
    n_down = send(values, nv.at[1], at(-1))
    c_up = send(cs, nc.at[0], at(1))
    c_down = send(cs, nc.at[1], at(-1))

    get_basis.wait()
    b_hi, b_lo = split(bas[...])
    oh_b[:, :RANK] = b_hi
    oh_b[:, RANK:] = b_lo
    order = perm[...] % LEAF

    def place(i, carry):
        row = pl.multiple_of(i * ROWS, ROWS)
        point = lax.broadcasted_iota(jnp.int32, (ROWS, LEAF), 0) + row
        hot = jnp.where(point == order, 1.0, 0.0).astype(BF16)
        moved = dot(hot, oh_b[...])
        bt_hi[pl.ds(row, ROWS), :] = moved[:, :RANK].astype(BF16)
        bt_lo[pl.ds(row, ROWS), :] = moved[:, RANK:].astype(BF16)
        return carry

    lax.fori_loop(0, LEAF // ROWS, place, 0)
    get_values.wait()
    v_hi, v_lo = split(val[...])
    vst[:, :NCOL] = v_hi
    vst[:, NCOL:] = v_lo
    vt_hi, vt_lo = split(val[...].T)
    c0_t = dot3((vt_hi, vt_lo), (bt_hi[...], bt_lo[...]))
    c0[...] = c0_t
    s0_up = send(c0, r0.at[0], at(2))
    s0_down = send(c0, r0.at[2], at(-2))
    get_e1.wait()
    t1_t = dot3(split(c0_t), split(e1[...]))
    t1[...] = t1_t
    s1 = send(t1, t1r, p1)

    def near(block, points, scaled, first, count):
        def step(i, carry):
            row = pl.multiple_of(i * ROWS, ROWS)
            own = pc[pl.ds(row, ROWS), :]
            total = None
            for j in range(0, LEAF, 256):
                far = None
                for axis in range(3):
                    gap = own[:, axis:axis + 1] - points[axis:axis + 1, j:j + 256]
                    far = gap * gap if far is None else far + gap * gap
                k_hi, k_lo = split(jnp.exp2(-far))
                both = block[j:j + 256, :]
                term = dot(k_hi, both)
                part = term[:, :NCOL] + term[:, NCOL:] + dot(k_lo, both[:, :NCOL])
                total = part if total is None else total + part
            if scaled is None:
                out[pl.ds(row, ROWS), :] = total
            else:
                out[pl.ds(row, ROWS), :] += total * scaled
            return carry

        lax.fori_loop(first, first + count, step, 0)

    near(vst, cs, None, 0, 1)

    s1.wait_recv()
    c1_t = t1[...] + t1r[...]
    c1[...] = jnp.where(core == 0, c1_t[:, :128], c1_t[:, 128:])
    s2_up = send(c1, r1.at[0], at(4))
    s2_down = send(c1, r1.at[2], at(-4))
    get_e2.wait()
    e2_near.wait_recv()
    get_e3.wait()
    e3_far.wait_recv()
    other = pl.multiple_of((quarter + 2 - 4 * (quarter // 2)) * 64, 64)
    e3_relay = send(e3.at[pl.ds(other, 64)], e3.at[pl.ds(other, 64)], p1)
    t2_t = dot3(split(c1_t), split(e2[...]))
    t2[...] = t2_t.T
    u2 = send(t2.at[pl.ds(other, 64)], t2r, p2)
    e3_near.wait_recv()
    e3_relay.wait_recv()
    t3_t = dot3(split(t2_t), split(e3[...]))
    t3[...] = t3_t.T
    u3 = []
    for n, peer in enumerate((p2, p4, p6)):
        piece = pl.multiple_of(peer % 8 * 32, 32)
        u3.append(send(t3.at[pl.ds(piece, 32)], t3r.at[n], peer))

    near(vst, cs, None, 1, 1)

    for copy in u3:
        copy.wait_recv()
    c3[...] = (t3[pl.ds(pl.multiple_of(eighth * 32, 32), 32), :] + t3r[0]) + (t3r[1] + t3r[2])
    s4_up = send(c3, r3.at[1], at(24))
    s4_down = send(c3, r3.at[3], at(-24))
    u2.wait_recv()
    c2[...] = t2[pl.ds(pl.multiple_of(quarter * 64, 64), 64), :] + t2r[...]
    s3_up = send(c2, r2.at[0], at(8))
    s3_down = send(c2, r2.at[2], at(-8))

    near(vst, cs, None, 2, 2)

    s4_up.wait_recv()
    f4_down = send(r3.at[1], r3.at[0], at(-8))
    s4_down.wait_recv()
    f4_up = send(r3.at[3], r3.at[2], at(8))
    s3_up.wait_recv()
    f3_up = send(r2.at[0], r2.at[1], at(4))
    s3_down.wait_recv()
    f3_down = send(r2.at[2], r2.at[3], at(-4))
    s2_up.wait_recv()
    f2_up = send(r1.at[0], r1.at[1], at(2))
    s2_down.wait_recv()
    f2_down = send(r1.at[2], r1.at[3], at(-2))
    s0_up.wait_recv()
    f0_up = send(r0.at[0], r0.at[1], at(1))
    s0_down.wait_recv()
    f0_down = send(r0.at[2], r0.at[3], at(-1))

    n_up.wait_recv()
    c_up.wait_recv()
    w_hi, w_lo = split(nv[0])
    nst[0, :, :NCOL] = w_hi
    nst[0, :, NCOL:] = w_lo
    has_left = jnp.where(me > 0, 1.0, 0.0)
    has_right = jnp.where(me < N_LEAF - 1, 1.0, 0.0)
    near(nst.at[0], nc.at[0], has_left, 0, 4)

    def choose(buf, level, slot):
        delta = inter[slot, level] - me // 2 ** level
        return jnp.where(
            delta == -2, buf[0], jnp.where(delta == -3, buf[1], jnp.where(delta == 2, buf[2], buf[3]))
        )

    def halves(y, level):
        keep = pl.multiple_of(core * 64, 64)
        give = pl.multiple_of((1 - core) * 64, 64)
        yh[level - 1] = y
        return keep, send(yh.at[level - 1, pl.ds(give, 64)], yhr.at[level - 1], p1)

    get_cpl.wait()
    f4_down.wait_recv()
    f4_up.wait_recv()
    both3 = jnp.concatenate([choose(r3, 3, 0), choose(r3, 3, 1)], axis=0).T
    y3 = dot3(split(both3), split(cpl[pl.ds(896, 64), :])) * 2.0 ** -1.5
    keep, d3 = halves(y3, 3)
    f3_up.wait_recv()
    f3_down.wait_recv()
    both2 = jnp.concatenate([choose(r2, 2, 0), choose(r2, 2, 1)], axis=0).T
    y2 = dot3(split(both2), split(cpl[pl.ds(768, 128), :])) * 0.5
    keep, d2 = halves(y2, 2)

    d3.wait_recv()
    h3[...] = yh[2, pl.ds(keep, 64), :] + yhr[2]
    q3 = []
    for n, peer in enumerate((p2, p4, p6)):
        piece = pl.multiple_of(peer // 2 % 4 * 16, 16)
        q3.append(send(h3.at[pl.ds(piece, 16)], h3r.at[n], peer))
    d2.wait_recv()
    h2[...] = yh[1, pl.ds(keep, 64), :] + yhr[1]
    q2 = send(h2, h2r, p2)

    n_down.wait_recv()
    c_down.wait_recv()
    w_hi, w_lo = split(nv[1])
    nst[1, :, :NCOL] = w_hi
    nst[1, :, NCOL:] = w_lo
    near(nst.at[1], nc.at[1], has_right, 0, 2)

    for copy in q3:
        copy.wait_recv()
    mine = pl.multiple_of(me // 2 % 4 * 16, 16)
    f3[pl.ds(mine, 16), :] = (h3[pl.ds(mine, 16), :] + h3r[0]) + (h3r[1] + h3r[2])
    g3 = []
    for peer in (p2, p4, p6):
        g3.append(send(f3.at[pl.ds(mine, 16)], f3.at[pl.ds(mine, 16)], peer))

    f2_up.wait_recv()
    f2_down.wait_recv()
    both1 = jnp.concatenate([choose(r1, 1, 0), choose(r1, 1, 1)], axis=1)
    y1 = dot3(split(both1), split(cpl[pl.ds(512, 256), :])) * 2.0 ** -0.5
    keep, d1 = halves(y1, 1)
    f0_up.wait_recv()
    f0_down.wait_recv()
    both0 = jnp.concatenate([choose(r0, 0, 0), choose(r0, 0, 1)], axis=1)
    y0[...] = dot3(split(both0), split(cpl[pl.ds(0, 512), :]))

    near(nst.at[1], nc.at[1], has_right, 2, 2)

    q2.wait_recv()
    for copy in g3:
        copy.wait_recv()
    d1.wait_recv()
    f2_t = (h2[...] + h2r[...]) + dot3(split(f3[...]), split(e3[...]), NT)
    f1_half = (yh[0, pl.ds(keep, 64), :] + yhr[0]) + dot3(split(f2_t), split(e2[...]), NT)
    f1[pl.ds(keep, 64), :] = f1_half
    g1 = send(f1.at[pl.ds(keep, 64)], f1.at[pl.ds(keep, 64)], p1)
    g1.wait_recv()
    f0 = y0[...] + dot3(split(f1[...]), split(e1[...]), NT)
    f0_s = split(f0)

    def finish(i, carry):
        row = pl.multiple_of(i * ROWS, ROWS)
        rows = (bt_hi[pl.ds(row, ROWS), :], bt_lo[pl.ds(row, ROWS), :])
        out[pl.ds(row, ROWS), :] += dot3(rows, f0_s, NT)
        return carry

    lax.fori_loop(0, LEAF // ROWS, finish, 0)
    for copy in used:
        copy.wait_send()


def per_device(values, coords, permutation, basis, transfers, couplings, interactions):
    vmem = pl.BlockSpec(memory_space=pltpu.VMEM)
    smem = pl.BlockSpec(memory_space=pltpu.SMEM)
    hbm = pl.BlockSpec(memory_space=pl.ANY)

    def f32(*shape):
        return pltpu.VMEM(shape, F32)

    def b16(*shape):
        return pltpu.VMEM(shape, BF16)

    copies = 48
    return pl.pallas_call(
        kernel,
        out_shape=jax.ShapeDtypeStruct((LEAF, NCOL), F32),
        in_specs=[hbm, vmem, vmem, hbm, hbm, hbm, smem],
        out_specs=vmem,
        scratch_shapes=[
            f32(LEAF, NCOL), f32(LEAF, RANK), f32(256, 256), f32(256, 256), f32(256, 256),
            f32(960, 256), f32(8, LEAF), f32(LEAF, 8), b16(LEAF, 256), b16(2, LEAF, 256),
            f32(2, LEAF, NCOL), f32(2, 8, LEAF), b16(LEAF, 512), b16(LEAF, 256), b16(LEAF, 256),
            f32(128, 256), f32(128, 256), f32(128, 256), f32(128, 128),
            f32(256, 128), f32(64, 128), f32(256, 128), f32(3, 32, 128),
            f32(64, 128), f32(32, 128),
            f32(4, 128, 256), f32(4, 128, 128), f32(4, 64, 128), f32(4, 32, 128),
            f32(3, 128, 256), f32(3, 64, 256), f32(64, 256), f32(64, 256),
            f32(64, 256), f32(3, 16, 256), f32(64, 256), f32(128, 256), f32(128, 256),
            pltpu.SemaphoreType.DMA((6,)),
            pltpu.SemaphoreType.DMA((copies,)),
            pltpu.SemaphoreType.DMA((copies,)),
        ],
        compiler_params=pltpu.CompilerParams(
            collective_id=0, has_side_effects=True, vmem_limit_bytes=48 * 2 ** 20
        ),
        cost_estimate=pl.CostEstimate(
            flops=3 * 2 ** 30, bytes_accessed=4 * 2 ** 20, transcendentals=3 * 2 ** 20
        ),
    )(
        values, coords, permutation.reshape(1, LEAF), basis, transfers, couplings,
        interactions.transpose(0, 2, 1).reshape(2, 4),
    )


def solution(mesh):
    in_specs = (
        P("leaf", None),
        P(None, "leaf"),
        P("leaf"),
        P("leaf", None),
        P("leaf", None),
        P("leaf", None),
        P("leaf", None, None),
    )
    out_specs = P("leaf", None)
    return jax.shard_map(
        per_device, mesh=mesh, in_specs=in_specs, out_specs=out_specs, check_vma=False
    )
```

time: 203 us -> 74.9 us (0.37)
  the two profiles are of different devices: /device:TPU:24 before, /device:TPU:1 now
where the time goes in v1:
time: 74.9 us; the launch traced here: 74.5 us
  Pallas kernels  67.1 us (90%)
  local copies, waits for them, and re-layouts  7.36 us (10%)
    pallas_call x1, Pallas kernels, per_device(): pl.pallas_call(kernel, out_shape=jax.ShapeDtypeStruct((LEAF, NCOL), F32),...  67.1 us
    unnamed x15, local copies, waits for them, and re-layouts  7.36 us

profile of v1, /device:TPU:1, one launch (start us, length us, event | category | flops | bytes accessed | tf_op | source)
XLA Modules:
  0.0 74.5 jit_solution(8799245763410491501)
XLA Ops:
  0.0 0.0 copy-start.6
  0.0 0.7 copy-done.6
  0.7 0.0 copy-start
  0.7 1.2 %copy-done = f32[1024,256]{1,0:T(8,128)S(1)} copy-done((f32[1024,256]{1,0:T(8,128)S(1)}, f32[1024,256]{1,0:T(8,128)}, u32[]{:S(2)}) %copy-start) | copy-done | bytes 1048600
  1.9 0.0 copy-start.1
  1.9 1.2 %copy-done.1 = f32[960,256]{1,0:T(8,128)S(1)} copy-done((f32[960,256]{1,0:T(8,128)S(1)}, f32[960,256]{1,0:T(8,128)}, u32[]{:S(2)}) %copy-start.1) | copy-done | bytes 983064
  3.1 0.0 copy-start.2
  3.1 1.0 %copy-done.2 = f32[1024,128]{1,0:T(8,128)S(1)} copy-done((f32[1024,128]{1,0:T(8,128)S(1)}, f32[1024,128]{1,0:T(8,128)}, u32[]{:S(2)}) %copy-start.2) | copy-done | bytes 524312
  4.1 0.0 copy-start.3
  4.2 1.0 %copy-done.3 = f32[448,256]{1,0:T(8,128)S(1)} copy-done((f32[448,256]{1,0:T(8,128)S(1)}, f32[448,256]{1,0:T(8,128)}, u32[]{:S(2)}) %copy-start.3) | copy-done | bytes 458776
  5.2 0.0 copy-start.4
  5.2 0.7 copy-done.4
  5.9 0.0 copy-start.5
  5.9 0.7 copy-done.5
  6.6 67.1 %shard_map.73 = f32[1024,128]{1,0:T(8,128)S(1)} custom-call(f32[1024,128]{1,0:T(8,128)S(1)} %copy-done.2, f32[3,1024]{1,0:T(4,128)S(1)} %copy-done.4, s32[1,1024]{1,0:T(1,128)S(1)} %bitcast.4, f32[1024,256]{1,0:T(8,128)S(1)} %copy-done, f32[448,256]{1,0:T(8,128)S(1)} %copy-done.3, f32[960,256]{1,0:T(8,128)S(1)} %copy-done.1, s32[2,4]{1,0:T(2,128)S(1)} %bitcast.5), custom_call_target="tpu_custom_call" | custom-call | flops 3221225472 | bytes 4194304 | tf_op jit(solution)/shard_map/pallas_call | solution.py:322
  73.7 0.8 %copy.9 = f32[1024,128]{1,0:T(8,128)} copy(f32[1024,128]{1,0:T(8,128)S(1)} %shard_map.73) | data formatting | bytes 1048576
Async XLA Ops:
  0.0 0.7 copy-start.6
  0.7 1.2 %copy-start = (f32[1024,256]{1,0:T(8,128)S(1)}, f32[1024,256]{1,0:T(8,128)}, u32[]{:S(2)}) copy-start(f32[1024,256]{1,0:T(8,128)} %basis.1) | copy-start | bytes 3145732
  1.9 1.2 %copy-start.1 = (f32[960,256]{1,0:T(8,128)S(1)}, f32[960,256]{1,0:T(8,128)}, u32[]{:S(2)}) copy-start(f32[960,256]{1,0:T(8,128)} %couplings.1) | copy-start | bytes 2949124
  3.1 1.0 %copy-start.2 = (f32[1024,128]{1,0:T(8,128)S(1)}, f32[1024,128]{1,0:T(8,128)}, u32[]{:S(2)}) copy-start(f32[1024,128]{1,0:T(8,128)} %values.1) | copy-start | bytes 1572868
  4.1 1.0 %copy-start.3 = (f32[448,256]{1,0:T(8,128)S(1)}, f32[448,256]{1,0:T(8,128)}, u32[]{:S(2)}) copy-start(f32[448,256]{1,0:T(8,128)} %transfers.1) | copy-start | bytes 1376260
  5.2 0.7 copy-start.4
  5.9 0.7 copy-start.5

commit v2 on v1

v2 whole, which is shorter than its diff:
```python
import functools
import math

import jax
import jax.numpy as jnp
from jax import lax
from jax.experimental import pallas as pl
from jax.experimental.pallas import tpu as pltpu
from jax.sharding import PartitionSpec as P

LEAF = 1024
RANK = 256
NCOL = 128
N_LEAF = 512
ROWS = 256
MESH = pl.DeviceIdType.MESH
F32 = jnp.float32
BF16 = jnp.bfloat16
NT = (((1,), (1,)), ((), ()))
NN = (((1,), (0,)), ((), ()))
SCALE = math.sqrt(8.0 * math.log2(math.e))


def split(x):
    hi = x.astype(BF16)
    return hi, (x - hi.astype(F32)).astype(BF16)


def dot(a, b, dims=NN):
    return lax.dot_general(a, b, dims, preferred_element_type=F32)


def dot3(a, b, dims=NN):
    a_hi, a_lo = a
    b_hi, b_lo = b
    return dot(a_hi, b_hi, dims) + (dot(a_hi, b_lo, dims) + dot(a_lo, b_hi, dims))


def kernel(
    values, coords_in, perm_in, basis, transfers, couplings, inter, out,
    coords, perm,
    val, bas, e1, e2, e3, cp0, cw, cs, pc, vst, nst, nv, nc, oh_b, bt_hi, bt_lo,
    c0, t1, t1r, c1, t2, t2r, t3, t3r, c2, c3, r0, r1, r2, r3,
    h2, h2r, h3, h3r, f3, f1, y0, y1,
    loc, snd, rcv,
):
    me = lax.axis_index("leaf")
    core = me % 2
    quarter = me % 4
    pair = me // 2 % 2
    chip = me // 2 % 4

    def at(offset):
        return (me + offset + N_LEAF) % N_LEAF

    p1 = me + 1 - 2 * core
    p2 = me + 2 - 4 * (me // 2 % 2)
    p4 = me + 4 - 8 * (me // 4 % 2)
    p6 = p2 + 4 - 8 * (me // 4 % 2)
    p3 = p2 + 1 - 2 * core

    barrier = pltpu.get_barrier_semaphore()

    def inside(offset):
        return (me + offset >= 0) & (me + offset < N_LEAF)

    def greet(peer):
        pl.semaphore_signal(barrier, inc=1, device_id=(peer,), device_id_type=MESH)

    group = (p1, p2, p3, p4, p6)
    for peer in group:
        greet(peer)
    expected = len(group)
    for offset in (1, -1, 2, -2, 4, -4, 8, -8, 16, -16, 24, -24):
        pl.when(inside(offset))(functools.partial(greet, at(offset)))
        expected = expected + jnp.where(inside(offset), 1, 0)

    local = []

    def bring(src, dst):
        copy = pltpu.make_async_copy(src, dst, loc.at[len(local)])
        copy.start()
        local.append(copy)
        return copy

    e2_row = pl.multiple_of(core * 128, 128)
    e3_row = pl.multiple_of(quarter * 64, 64)
    get_coords = bring(coords_in, coords)
    get_perm = bring(perm_in, perm)
    get_basis = bring(basis, bas)
    get_values = bring(values, val)
    get_e1 = bring(transfers.at[pl.ds(0, 256)], e1)
    get_e2 = bring(transfers.at[pl.ds(256, 128)], e2.at[pl.ds(e2_row, 128)])
    get_e3 = bring(transfers.at[pl.ds(384, 64)], e3.at[pl.ds(e3_row, 64)])
    get_cp0 = bring(couplings.at[pl.ds(0, 512)], cp0)
    get_cw = bring(couplings.at[pl.ds(512, 448)], cw.at[core])

    get_coords.wait()
    cs[pl.ds(0, 3), :] = coords[...] * SCALE
    cs[pl.ds(3, 5), :] = jnp.zeros((5, LEAF), F32)
    pc[...] = cs[...].T

    get_basis.wait()
    b_hi, b_lo = split(bas[...])
    oh_b[:, :RANK] = b_hi
    oh_b[:, RANK:] = b_lo
    get_perm.wait()
    order = perm[...] % LEAF

    def place(i, carry):
        row = pl.multiple_of(i * ROWS, ROWS)
        point = lax.broadcasted_iota(jnp.int32, (ROWS, LEAF), 0) + row
        hot = jnp.where(point == order, 1.0, 0.0).astype(BF16)
        moved = dot(hot, oh_b[...])
        bt_hi[pl.ds(row, ROWS), :] = moved[:, :RANK].astype(BF16)
        bt_lo[pl.ds(row, ROWS), :] = moved[:, RANK:].astype(BF16)
        return carry

    lax.fori_loop(0, LEAF // ROWS, place, 0)
    get_values.wait()
    v_hi, v_lo = split(val[...])
    vst[:, :NCOL] = v_hi
    vst[:, NCOL:] = v_lo
    vt_hi, vt_lo = split(val[...].T)
    c0_t = dot3((vt_hi, vt_lo), (bt_hi[...], bt_lo[...]))
    c0[...] = c0_t
    get_e1.wait()
    t1_t = dot3(split(c0_t), split(e1[...]))
    t1[...] = t1_t
    get_e2.wait()
    get_e3.wait()
    get_cp0.wait()
    get_cw.wait()

    pl.semaphore_wait(barrier, expected)

    used = []

    class Sent:
        def __init__(self, copy, goes, comes):
            self.copy, self.goes, self.comes = copy, goes, comes

        def wait_recv(self):
            if self.comes is None:
                self.copy.wait_recv()
            else:
                pl.when(self.comes)(self.copy.wait_recv)

        def wait_send(self):
            if self.goes is None:
                self.copy.wait_send()
            else:
                pl.when(self.goes)(self.copy.wait_send)

    def send(src, dst, peer, goes=None, comes=None):
        index = len(used)
        copy = pltpu.make_async_remote_copy(
            src_ref=src, dst_ref=dst, send_sem=snd.at[index], recv_sem=rcv.at[index],
            device_id=(peer,), device_id_type=MESH,
        )
        if goes is None:
            copy.start()
        else:
            pl.when(goes)(copy.start)
        used.append(Sent(copy, goes, comes))
        return used[-1]

    def shift(src, dst, offset):
        return send(src, dst, at(offset), inside(offset), inside(-offset))

    def relay(src, dst, offset):
        return send(
            src, dst, at(offset), inside(-2 * offset) & inside(offset), inside(-3 * offset)
        )

    def share(piece):
        rows = pl.ds(piece * 256, 256)
        return (
            shift(values.at[rows], nv.at[0, rows], 1),
            shift(values.at[rows], nv.at[1, rows], -1),
        )

    def near(block, points, piece, fresh):
        j = piece * 256

        def step(i, carry):
            row = pl.multiple_of(i * ROWS, ROWS)
            own = pc[pl.ds(row, ROWS), :]
            far = None
            for axis in range(3):
                gap = own[:, axis:axis + 1] - points[axis:axis + 1, j:j + 256]
                far = gap * gap if far is None else far + gap * gap
            k_hi, k_lo = split(jnp.exp2(-far))
            both = block[j:j + 256, :]
            term = dot(k_hi, both)
            total = term[:, :NCOL] + term[:, NCOL:] + dot(k_lo, both[:, :NCOL])
            if fresh:
                out[pl.ds(row, ROWS), :] = total
            else:
                out[pl.ds(row, ROWS), :] += total
            return carry

        lax.fori_loop(0, LEAF // ROWS, step, 0)

    def near_side(side, sent, piece):
        def work():
            rows = pl.ds(piece * 256, 256)
            w_hi, w_lo = split(nv[side, rows, :])
            nst[side, rows, :NCOL] = w_hi
            nst[side, rows, NCOL:] = w_lo
            near(nst.at[side], nc.at[side], piece, False)

        sent[side].wait_recv()
        pl.when(inside(-1 if side == 0 else 1))(work)


    def choose(buf, level, slot):
        delta = inter[slot, level] - me // 2 ** level
        return jnp.where(
            delta == -2, buf[0], jnp.where(delta == -3, buf[1], jnp.where(delta == 2, buf[2], buf[3]))
        )

    def coupled(buf, level, first, count):
        both = jnp.concatenate([choose(buf, level, 0), choose(buf, level, 1)], axis=0).T
        rows = pl.ds(first, count)
        return (
            dot3(split(both[:64]), split(cw[0, rows, :]))
            + dot3(split(both[64:]), split(cw[1, rows, :]))
        ) * 2.0 ** (-level / 2.0)

    keep = pl.multiple_of(core * 64, 64)
    give = pl.multiple_of((1 - core) * 64, 64)
    e3_own = e3.at[pl.ds(e3_row, 64)]
    s1 = send(t1.at[pl.ds(give, 64)], t1r, p1)
    e2_near = send(transfers.at[pl.ds(256, 128)], e2.at[pl.ds(e2_row, 128)], p1)
    e3_far = send(transfers.at[pl.ds(384, 64)], e3_own, p2)
    e3_near = send(transfers.at[pl.ds(384, 64)], e3_own, p1)
    s0_up = shift(c0, r0.at[0], 2)
    s0_down = shift(c0, r0.at[2], -2)
    cw_near = send(couplings.at[pl.ds(512, 448)], cw.at[core], p1)
    c_up = shift(cs, nc.at[0], 1)
    c_down = shift(cs, nc.at[1], -1)
    near(vst, cs, 0, True)

    s1.wait_recv()
    c1_t = t1[pl.ds(keep, 64), :] + t1r[...]
    c1[...] = c1_t
    e2_near.wait_recv()
    t2_t = dot3(split(c1_t), split(e2[...]))
    t2_q = t2_t.T
    for b in range(2):
        t2[b] = jnp.concatenate([t2_q[b * 128:b * 128 + 64], t2_q[b * 128 + 64:b * 128 + 128]], axis=1)
    u2 = send(t2.at[1 - pair], t2r, p2)
    near(vst, cs, 1, False)
    e3_far.wait_recv()
    other = pl.multiple_of((quarter + 2 - 4 * (quarter // 2)) * 64, 64)
    e3_relay = send(e3.at[pl.ds(other, 64)], e3.at[pl.ds(other, 64)], p1)
    near(vst, cs, 2, False)
    e3_near.wait_recv()
    e3_relay.wait_recv()
    t3_t = dot3(split(t2_t), split(e3[...]))
    t3_q = t3_t.T
    for b in range(4):
        t3[b] = jnp.concatenate([t3_q[b * 64:b * 64 + 32], t3_q[b * 64 + 32:b * 64 + 64]], axis=1)
    u3 = []
    for n, peer in enumerate((p2, p4, p6)):
        u3.append(send(t3.at[peer // 2 % 4], t3r.at[n], peer))

    s2_up = shift(c1, r1.at[0], 4)
    s2_down = shift(c1, r1.at[2], -4)
    near(vst, cs, 3, False)
    s0_up.wait_recv()
    f0_up = relay(r0.at[0], r0.at[1], 1)
    s0_down.wait_recv()
    f0_down = relay(r0.at[2], r0.at[3], -1)
    u2.wait_recv()
    c2[...] = t2[pair] + t2r[...]
    for copy in u3:
        copy.wait_recv()
    c3[...] = (t3[chip] + t3r[0]) + (t3r[1] + t3r[2])
    s4 = [
        shift(c3, r3.at[0], 16), shift(c3, r3.at[2], -16),
        shift(c3, r3.at[1], 24), shift(c3, r3.at[3], -24),
    ]

    s3_up = shift(c2, r2.at[0], 8)
    s3_down = shift(c2, r2.at[2], -8)
    v0 = share(0)
    s2_up.wait_recv()
    f2_up = relay(r1.at[0], r1.at[1], 2)
    s2_down.wait_recv()
    f2_down = relay(r1.at[2], r1.at[3], -2)
    f0_up.wait_recv()
    f0_down.wait_recv()
    both0 = jnp.concatenate([choose(r0, 0, 0), choose(r0, 0, 1)], axis=1)
    y0[...] = dot3(split(both0), split(cp0[...]))

    s3_up.wait_recv()
    f3_up = relay(r2.at[0], r2.at[1], 4)
    s3_down.wait_recv()
    f3_down = relay(r2.at[2], r2.at[3], -4)
    c_up.wait_recv()
    c_down.wait_recv()
    cw_near.wait_recv()
    near_side(0, v0, 0)
    for copy in s4:
        copy.wait_recv()
    h3[...] = coupled(r3, 3, 384, 64)
    q3 = []
    for n, peer in enumerate((p2, p4, p6)):
        piece = pl.multiple_of(peer // 2 % 4 * 16, 16)
        q3.append(send(h3.at[pl.ds(piece, 16)], h3r.at[n], peer))

    v1 = share(1)
    v2 = share(2)
    near_side(1, v0, 0)
    f3_up.wait_recv()
    f3_down.wait_recv()
    h2[...] = coupled(r2, 2, 256, 128)
    q2 = send(h2, h2r, p2)
    f2_up.wait_recv()
    f2_down.wait_recv()
    both1 = jnp.concatenate([choose(r1, 1, 0), choose(r1, 1, 1)], axis=1)
    rows1 = jnp.concatenate(
        [cw[0, pl.ds(0, 128), :], cw[1, pl.ds(0, 128), :], cw[0, pl.ds(128, 128), :], cw[1, pl.ds(128, 128), :]],
        axis=0,
    )
    y1[...] = dot3(split(both1), split(rows1)) * 2.0 ** -0.5
    for copy in q3:
        copy.wait_recv()
    mine = pl.multiple_of(chip * 16, 16)
    f3[pl.ds(mine, 16), :] = (h3[pl.ds(mine, 16), :] + h3r[0]) + (h3r[1] + h3r[2])
    g3 = []
    for peer in (p2, p4, p6):
        g3.append(send(f3.at[pl.ds(mine, 16)], f3.at[pl.ds(mine, 16)], peer))

    v3 = share(3)
    near_side(0, v1, 1)
    near_side(1, v1, 1)
    near_side(0, v2, 2)
    near_side(1, v2, 2)
    q2.wait_recv()
    for copy in g3:
        copy.wait_recv()
    f2_t = (h2[...] + h2r[...]) + dot3(split(f3[...]), split(e3[...]), NT)
    f1_half = y1[...] + dot3(split(f2_t), split(e2[...]), NT)
    f1[pl.ds(keep, 64), :] = f1_half
    g1 = send(f1.at[pl.ds(keep, 64)], f1.at[pl.ds(keep, 64)], p1)
    near_side(0, v3, 3)
    near_side(1, v3, 3)
    g1.wait_recv()
    f0 = y0[...] + dot3(split(f1[...]), split(e1[...]), NT)
    f0_s = split(f0)

    def finish(i, carry):
        row = pl.multiple_of(i * ROWS, ROWS)
        rows = (bt_hi[pl.ds(row, ROWS), :], bt_lo[pl.ds(row, ROWS), :])
        out[pl.ds(row, ROWS), :] += dot3(rows, f0_s, NT)
        return carry

    lax.fori_loop(0, LEAF // ROWS, finish, 0)
    for copy in used:
        copy.wait_send()


def per_device(values, coords, permutation, basis, transfers, couplings, interactions):
    vmem = pl.BlockSpec(memory_space=pltpu.VMEM)
    smem = pl.BlockSpec(memory_space=pltpu.SMEM)
    hbm = pl.BlockSpec(memory_space=pltpu.HBM)

    def f32(*shape):
        return pltpu.VMEM(shape, F32)

    def b16(*shape):
        return pltpu.VMEM(shape, BF16)

    copies = 64
    return pl.pallas_call(
        kernel,
        out_shape=jax.ShapeDtypeStruct((LEAF, NCOL), F32),
        in_specs=[hbm, hbm, hbm, hbm, hbm, hbm, smem],
        out_specs=vmem,
        scratch_shapes=[
            f32(3, LEAF), pltpu.VMEM((1, LEAF), jnp.int32),
            f32(LEAF, NCOL), f32(LEAF, RANK), f32(256, 256), f32(256, 256), f32(256, 256),
            f32(512, 256), f32(2, 448, 256), f32(8, LEAF), f32(LEAF, 8), b16(LEAF, 256), b16(2, LEAF, 256),
            f32(2, LEAF, NCOL), f32(2, 8, LEAF), b16(LEAF, 512), b16(LEAF, 256), b16(LEAF, 256),
            f32(128, 256), f32(128, 256), f32(64, 256), f32(64, 256),
            f32(2, 64, 128), f32(64, 128), f32(4, 32, 128), f32(3, 32, 128),
            f32(64, 128), f32(32, 128),
            f32(4, 128, 256), f32(4, 64, 256), f32(4, 64, 128), f32(4, 32, 128),
            f32(64, 256), f32(64, 256), f32(64, 256), f32(3, 16, 256), f32(64, 256),
            f32(128, 256), f32(128, 256), f32(64, 256),
            pltpu.SemaphoreType.DMA((9,)),
            pltpu.SemaphoreType.DMA((copies,)),
            pltpu.SemaphoreType.DMA((copies,)),
        ],
        compiler_params=pltpu.CompilerParams(
            collective_id=0, has_side_effects=True, vmem_limit_bytes=63 * 2 ** 20
        ),
        cost_estimate=pl.CostEstimate(
            flops=3 * 2 ** 30, bytes_accessed=4 * 2 ** 20, transcendentals=3 * 2 ** 20
        ),
    )(
        values, coords, permutation.reshape(1, LEAF), basis, transfers, couplings,
        interactions.transpose(0, 2, 1).reshape(2, 4),
    )


def solution(mesh):
    in_specs = (
        P("leaf", None),
        P(None, "leaf"),
        P("leaf"),
        P("leaf", None),
        P("leaf", None),
        P("leaf", None),
        P("leaf", None, None),
    )
    out_specs = P("leaf", None)
    return jax.shard_map(
        per_device, mesh=mesh, in_specs=in_specs, out_specs=out_specs, check_vma=False
    )
```

time: 74.9 us -> 61.4 us (0.82)
  the two profiles are of different devices: /device:TPU:1 before, /device:TPU:24 now
where the time goes in v2:
time: 61.4 us; the launch traced here: 61.2 us
  Pallas kernels  59.3 us (97%)
  local copies, waits for them, and re-layouts  1.87 us (3%)
    pallas_call x1, Pallas kernels, per_device(): pl.pallas_call(kernel, out_shape=jax.ShapeDtypeStruct((LEAF, NCOL), F32),...  59.3 us
    unnamed x1, local copies, waits for them, and re-layouts  1.87 us

profile of v2, /device:TPU:24, one launch (start us, length us, event | category | flops | bytes accessed | tf_op | source)
XLA Modules:
  0.0 61.2 jit_solution(2945470484539941411)
XLA Ops:
  0.0 59.3 %shard_map.73 = f32[1024,128]{1,0:T(8,128)} custom-call(f32[1024,128]{1,0:T(8,128)} %values.1, f32[3,1024]{1,0:T(4,128)} %coords_in.1, s32[1,1024]{1,0:T(1,128)} %bitcast.4, f32[1024,256]{1,0:T(8,128)} %basis.1, f32[448,256]{1,0:T(8,128)} %transfers.1, f32[960,256]{1,0:T(8,128)} %couplings.1, s32[2,4]{1,0:T(2,128)} %bitcast.5), custom_call_target="tpu_custom_call" | custom-call | flops 3221225472 | bytes 4194304 | tf_op jit(solution)/shard_map/pallas_call | solution.py:378
  59.4 1.9 %copy.9 = f32[1024,128]{1,0:T(8,128)} copy(f32[1024,128]{1,0:T(8,128)} %shard_map.73) | data formatting | bytes 1048576

commit v3 on v2

--- a/solution.py
+++ b/solution.py
@@ -39,7 +39,7 @@
 def kernel(
     values, coords_in, perm_in, basis, transfers, couplings, inter, out,
     coords, perm,
-    val, bas, e1, e2, e3, cp0, cw, cs, pc, vst, nst, nv, nc, oh_b, bt_hi, bt_lo,
+    val, bas, e1, e2, e3, cp0, cw, cs, pc, pb, vst, nst, nv, nc, oh_b, bt_hi, bt_lo,
     c0, t1, t1r, c1, t2, t2r, t3, t3r, c2, c3, r0, r1, r2, r3,
     h2, h2r, h3, h3r, f3, f1, y0, y1,
     loc, snd, rcv,
@@ -117,6 +117,112 @@
         return carry
 
     lax.fori_loop(0, LEAF // ROWS, place, 0)
+    pl.semaphore_wait(barrier, expected)
+
+    used = []
+
+    class Sent:
+        def __init__(self, copy, goes, comes):
+            self.copy, self.goes, self.comes = copy, goes, comes
+
+        def wait_recv(self):
+            if self.comes is None:
+                self.copy.wait_recv()
+            else:
+                pl.when(self.comes)(self.copy.wait_recv)
+
+        def wait_send(self):
+            if self.goes is None:
+                self.copy.wait_send()
+            else:
+                pl.when(self.goes)(self.copy.wait_send)
+
+    def send(src, dst, peer, goes=None, comes=None):
+        index = len(used)
+        copy = pltpu.make_async_remote_copy(
+            src_ref=src, dst_ref=dst, send_sem=snd.at[index], recv_sem=rcv.at[index],
+            device_id=(peer,), device_id_type=MESH,
+        )
+        if goes is None:
+            copy.start()
+        else:
+            pl.when(goes)(copy.start)
+        used.append(Sent(copy, goes, comes))
+        return used[-1]
+
+    def shift(src, dst, offset):
+        return send(src, dst, at(offset), inside(offset), inside(-offset))
+
+    def relay(src, dst, offset):
+        return send(
+            src, dst, at(offset), inside(-2 * offset) & inside(offset), inside(-3 * offset)
+        )
+
+    def share(piece):
+        rows = pl.ds(piece * 256, 256)
+        return (
+            shift(values.at[rows], nv.at[0, rows], 1),
+            shift(values.at[rows], nv.at[1, rows], -1),
+        )
+
+    def near(block, points, piece, fresh):
+        j = piece * 256
+
+        def step(i, carry):
+            row = pl.multiple_of(i * ROWS, ROWS)
+            far = None
+            for axis in range(3):
+                own = pb[axis, pl.ds(row, ROWS), :]
+                gap = jnp.concatenate([own, own], axis=1) - points[axis:axis + 1, j:j + 256]
+                far = gap * gap if far is None else far + gap * gap
+            k_hi, k_lo = split(jnp.exp2(-far))
+            both = block[j:j + 256, :]
+            term = dot(k_hi, both)
+            total = term[:, :NCOL] + term[:, NCOL:] + dot(k_lo, both[:, :NCOL])
+            if fresh:
+                out[pl.ds(row, ROWS), :] = total
+            else:
+                out[pl.ds(row, ROWS), :] += total
+            return carry
+
+        lax.fori_loop(0, LEAF // ROWS, step, 0)
+
+    def near_side(side, sent, piece):
+        def work():
+            rows = pl.ds(piece * 256, 256)
+            w_hi, w_lo = split(nv[side, rows, :])
+            nst[side, rows, :NCOL] = w_hi
+            nst[side, rows, NCOL:] = w_lo
+            near(nst.at[side], nc.at[side], piece, False)
+
+        sent[side].wait_recv()
+        pl.when(inside(-1 if side == 0 else 1))(work)
+
+
+    def choose(buf, level, slot):
+        delta = inter[slot, level] - me // 2 ** level
+        return jnp.where(
+            delta == -2, buf[0], jnp.where(delta == -3, buf[1], jnp.where(delta == 2, buf[2], buf[3]))
+        )
+
+    def coupled(buf, level, first, count):
+        both = jnp.concatenate([choose(buf, level, 0), choose(buf, level, 1)], axis=0).T
+        rows = pl.ds(first, count)
+        return (
+            dot3(split(both[:64]), split(cw[0, rows, :]))
+            + dot3(split(both[64:]), split(cw[1, rows, :]))
+        ) * 2.0 ** (-level / 2.0)
+
+    keep = pl.multiple_of(core * 64, 64)
+    give = pl.multiple_of((1 - core) * 64, 64)
+    e3_own = e3.at[pl.ds(e3_row, 64)]
+    e3_far = send(transfers.at[pl.ds(384, 64)], e3_own, p2)
+    e3_near = send(transfers.at[pl.ds(384, 64)], e3_own, p1)
+    e2_near = send(transfers.at[pl.ds(256, 128)], e2.at[pl.ds(e2_row, 128)], p1)
+    c_up = shift(cs, nc.at[0], 1)
+    c_down = shift(cs, nc.at[1], -1)
+    v0 = share(0)
+
     get_values.wait()
     v_hi, v_lo = split(val[...])
     vst[:, :NCOL] = v_hi
@@ -129,117 +235,13 @@
     t1[...] = t1_t
     get_e2.wait()
     get_e3.wait()
-    get_cp0.wait()
-    get_cw.wait()
-
-    pl.semaphore_wait(barrier, expected)
-
-    used = []
-
-    class Sent:
-        def __init__(self, copy, goes, comes):
-            self.copy, self.goes, self.comes = copy, goes, comes
-
-        def wait_recv(self):
-            if self.comes is None:
-                self.copy.wait_recv()
-            else:
-                pl.when(self.comes)(self.copy.wait_recv)
-
-        def wait_send(self):
-            if self.goes is None:
-                self.copy.wait_send()
-            else:
-                pl.when(self.goes)(self.copy.wait_send)
-
-    def send(src, dst, peer, goes=None, comes=None):
-        index = len(used)
-        copy = pltpu.make_async_remote_copy(
-            src_ref=src, dst_ref=dst, send_sem=snd.at[index], recv_sem=rcv.at[index],
-            device_id=(peer,), device_id_type=MESH,
-        )
-        if goes is None:
-            copy.start()
-        else:
-            pl.when(goes)(copy.start)
-        used.append(Sent(copy, goes, comes))
-        return used[-1]
-
-    def shift(src, dst, offset):
-        return send(src, dst, at(offset), inside(offset), inside(-offset))
-
-    def relay(src, dst, offset):
-        return send(
-            src, dst, at(offset), inside(-2 * offset) & inside(offset), inside(-3 * offset)
-        )
-
-    def share(piece):
-        rows = pl.ds(piece * 256, 256)
-        return (
-            shift(values.at[rows], nv.at[0, rows], 1),
-            shift(values.at[rows], nv.at[1, rows], -1),
-        )
-
-    def near(block, points, piece, fresh):
-        j = piece * 256
-
-        def step(i, carry):
-            row = pl.multiple_of(i * ROWS, ROWS)
-            own = pc[pl.ds(row, ROWS), :]
-            far = None
-            for axis in range(3):
-                gap = own[:, axis:axis + 1] - points[axis:axis + 1, j:j + 256]
-                far = gap * gap if far is None else far + gap * gap
-            k_hi, k_lo = split(jnp.exp2(-far))
-            both = block[j:j + 256, :]
-            term = dot(k_hi, both)
-            total = term[:, :NCOL] + term[:, NCOL:] + dot(k_lo, both[:, :NCOL])
-            if fresh:
-                out[pl.ds(row, ROWS), :] = total
-            else:
-                out[pl.ds(row, ROWS), :] += total
-            return carry
-
-        lax.fori_loop(0, LEAF // ROWS, step, 0)
-
-    def near_side(side, sent, piece):
-        def work():
-            rows = pl.ds(piece * 256, 256)
-            w_hi, w_lo = split(nv[side, rows, :])
-            nst[side, rows, :NCOL] = w_hi
-            nst[side, rows, NCOL:] = w_lo
-            near(nst.at[side], nc.at[side], piece, False)
-
-        sent[side].wait_recv()
-        pl.when(inside(-1 if side == 0 else 1))(work)
-
-
-    def choose(buf, level, slot):
-        delta = inter[slot, level] - me // 2 ** level
-        return jnp.where(
-            delta == -2, buf[0], jnp.where(delta == -3, buf[1], jnp.where(delta == 2, buf[2], buf[3]))
-        )
-
-    def coupled(buf, level, first, count):
-        both = jnp.concatenate([choose(buf, level, 0), choose(buf, level, 1)], axis=0).T
-        rows = pl.ds(first, count)
-        return (
-            dot3(split(both[:64]), split(cw[0, rows, :]))
-            + dot3(split(both[64:]), split(cw[1, rows, :]))
-        ) * 2.0 ** (-level / 2.0)
-
-    keep = pl.multiple_of(core * 64, 64)
-    give = pl.multiple_of((1 - core) * 64, 64)
-    e3_own = e3.at[pl.ds(e3_row, 64)]
+
     s1 = send(t1.at[pl.ds(give, 64)], t1r, p1)
-    e2_near = send(transfers.at[pl.ds(256, 128)], e2.at[pl.ds(e2_row, 128)], p1)
-    e3_far = send(transfers.at[pl.ds(384, 64)], e3_own, p2)
-    e3_near = send(transfers.at[pl.ds(384, 64)], e3_own, p1)
     s0_up = shift(c0, r0.at[0], 2)
     s0_down = shift(c0, r0.at[2], -2)
     cw_near = send(couplings.at[pl.ds(512, 448)], cw.at[core], p1)
-    c_up = shift(cs, nc.at[0], 1)
-    c_down = shift(cs, nc.at[1], -1)
+    for axis in range(3):
+        pb[axis] = jnp.broadcast_to(pc[:, axis:axis + 1], (LEAF, NCOL))
     near(vst, cs, 0, True)
 
     s1.wait_recv()
@@ -285,7 +287,12 @@
 
     s3_up = shift(c2, r2.at[0], 8)
     s3_down = shift(c2, r2.at[2], -8)
-    v0 = share(0)
+    c_up.wait_recv()
+    c_down.wait_recv()
+    get_cw.wait()
+    cw_near.wait_recv()
+    near_side(0, v0, 0)
+    near_side(1, v0, 0)
     s2_up.wait_recv()
     f2_up = relay(r1.at[0], r1.at[1], 2)
     s2_down.wait_recv()
@@ -293,16 +300,14 @@
     f0_up.wait_recv()
     f0_down.wait_recv()
     both0 = jnp.concatenate([choose(r0, 0, 0), choose(r0, 0, 1)], axis=1)
+    get_cp0.wait()
     y0[...] = dot3(split(both0), split(cp0[...]))
 
+    v1 = share(1)
     s3_up.wait_recv()
     f3_up = relay(r2.at[0], r2.at[1], 4)
     s3_down.wait_recv()
     f3_down = relay(r2.at[2], r2.at[3], -4)
-    c_up.wait_recv()
-    c_down.wait_recv()
-    cw_near.wait_recv()
-    near_side(0, v0, 0)
     for copy in s4:
         copy.wait_recv()
     h3[...] = coupled(r3, 3, 384, 64)
@@ -311,9 +316,8 @@
         piece = pl.multiple_of(peer // 2 % 4 * 16, 16)
         q3.append(send(h3.at[pl.ds(piece, 16)], h3r.at[n], peer))
 
-    v1 = share(1)
     v2 = share(2)
-    near_side(1, v0, 0)
+    near_side(0, v1, 1)
     f3_up.wait_recv()
     f3_down.wait_recv()
     h2[...] = coupled(r2, 2, 256, 128)
@@ -335,7 +339,6 @@
         g3.append(send(f3.at[pl.ds(mine, 16)], f3.at[pl.ds(mine, 16)], peer))
 
     v3 = share(3)
-    near_side(0, v1, 1)
     near_side(1, v1, 1)
     near_side(0, v2, 2)
     near_side(1, v2, 2)
@@ -350,12 +353,14 @@
     near_side(1, v3, 3)
     g1.wait_recv()
     f0 = y0[...] + dot3(split(f1[...]), split(e1[...]), NT)
-    f0_s = split(f0)
+    f0_hi, f0_lo = split(f0.T)
+    f0_both = jnp.concatenate([f0_hi, f0_lo], axis=1)
 
     def finish(i, carry):
         row = pl.multiple_of(i * ROWS, ROWS)
-        rows = (bt_hi[pl.ds(row, ROWS), :], bt_lo[pl.ds(row, ROWS), :])
-        out[pl.ds(row, ROWS), :] += dot3(rows, f0_s, NT)
+        first = dot(bt_hi[pl.ds(row, ROWS), :], f0_both)
+        second = dot(bt_lo[pl.ds(row, ROWS), :], f0_hi)
+        out[pl.ds(row, ROWS), :] += first[:, :NCOL] + (first[:, NCOL:] + second)
         return carry
 
     lax.fori_loop(0, LEAF // ROWS, finish, 0)
@@ -383,7 +388,7 @@
         scratch_shapes=[
             f32(3, LEAF), pltpu.VMEM((1, LEAF), jnp.int32),
             f32(LEAF, NCOL), f32(LEAF, RANK), f32(256, 256), f32(256, 256), f32(256, 256),
-            f32(512, 256), f32(2, 448, 256), f32(8, LEAF), f32(LEAF, 8), b16(LEAF, 256), b16(2, LEAF, 256),
+            f32(512, 256), f32(2, 448, 256), f32(8, LEAF), f32(LEAF, 8), f32(3, LEAF, NCOL), b16(LEAF, 256), b16(2, LEAF, 256),
             f32(2, LEAF, NCOL), f32(2, 8, LEAF), b16(LEAF, 512), b16(LEAF, 256), b16(LEAF, 256),
             f32(128, 256), f32(128, 256), f32(64, 256), f32(64, 256),
             f32(2, 64, 128), f32(64, 128), f32(4, 32, 128), f32(3, 32, 128),

time: 61.4 us -> 57.8 us (0.941)
  Pallas kernels: 59.3 us -> 55.7 us
    pallas_call x1, Pallas kernels: 59.3 us -> 55.7 us  [per_device(): pl.pallas_call(kernel, out_shape=jax.ShapeDtypeStruct((LEAF, NCOL), F32),...]
where the time goes in v3:
time: 57.8 us; the launch traced here: 57.6 us
  Pallas kernels  55.7 us (96%)
  local copies, waits for them, and re-layouts  1.87 us (3%)
    pallas_call x1, Pallas kernels, per_device(): pl.pallas_call(kernel, out_shape=jax.ShapeDtypeStruct((LEAF, NCOL), F32),...  55.7 us
    unnamed x1, local copies, waits for them, and re-layouts  1.87 us

profile of v3, /device:TPU:24, one launch (start us, length us, event | category | flops | bytes accessed | tf_op | source)
XLA Modules:
  0.0 57.6 jit_solution(15561050244881593319)
XLA Ops:
  0.0 55.7 %shard_map.73 = f32[1024,128]{1,0:T(8,128)} custom-call(f32[1024,128]{1,0:T(8,128)} %values.1, f32[3,1024]{1,0:T(4,128)} %coords_in.1, s32[1,1024]{1,0:T(1,128)} %bitcast.4, f32[1024,256]{1,0:T(8,128)} %basis.1, f32[448,256]{1,0:T(8,128)} %transfers.1, f32[960,256]{1,0:T(8,128)} %couplings.1, s32[2,4]{1,0:T(2,128)} %bitcast.5), custom_call_target="tpu_custom_call" | custom-call | flops 3221225472 | bytes 4194304 | tf_op jit(solution)/shard_map/pallas_call | solution.py:383
  55.7 1.9 %copy.9 = f32[1024,128]{1,0:T(8,128)} copy(f32[1024,128]{1,0:T(8,128)} %shard_map.73) | data formatting | bytes 1048576

commit v4 on v3

--- a/solution.py
+++ b/solution.py
@@ -41,7 +41,7 @@
     coords, perm,
     val, bas, e1, e2, e3, cp0, cw, cs, pc, pb, vst, nst, nv, nc, oh_b, bt_hi, bt_lo,
     c0, t1, t1r, c1, t2, t2r, t3, t3r, c2, c3, r0, r1, r2, r3,
-    h2, h2r, h3, h3r, f3, f1, y0, y1,
+    h2, h2r, h3, h3r, f3, f1, y0, y1, et,
     loc, snd, rcv,
 ):
     me = lax.axis_index("leaf")
@@ -219,8 +219,6 @@
     e3_far = send(transfers.at[pl.ds(384, 64)], e3_own, p2)
     e3_near = send(transfers.at[pl.ds(384, 64)], e3_own, p1)
     e2_near = send(transfers.at[pl.ds(256, 128)], e2.at[pl.ds(e2_row, 128)], p1)
-    c_up = shift(cs, nc.at[0], 1)
-    c_down = shift(cs, nc.at[1], -1)
     v0 = share(0)
 
     get_values.wait()
@@ -268,6 +266,8 @@
     for n, peer in enumerate((p2, p4, p6)):
         u3.append(send(t3.at[peer // 2 % 4], t3r.at[n], peer))
 
+    c_up = shift(cs, nc.at[0], 1)
+    c_down = shift(cs, nc.at[1], -1)
     s2_up = shift(c1, r1.at[0], 4)
     s2_down = shift(c1, r1.at[2], -4)
     near(vst, cs, 3, False)
@@ -289,8 +289,8 @@
     s3_down = shift(c2, r2.at[2], -8)
     c_up.wait_recv()
     c_down.wait_recv()
-    get_cw.wait()
-    cw_near.wait_recv()
+    for n, mat in enumerate((e1, e2, e3)):
+        et[2 * n], et[2 * n + 1] = split(mat[...].T)
     near_side(0, v0, 0)
     near_side(1, v0, 0)
     s2_up.wait_recv()
@@ -308,6 +308,8 @@
     f3_up = relay(r2.at[0], r2.at[1], 4)
     s3_down.wait_recv()
     f3_down = relay(r2.at[2], r2.at[3], -4)
+    get_cw.wait()
+    cw_near.wait_recv()
     for copy in s4:
         copy.wait_recv()
     h3[...] = coupled(r3, 3, 384, 64)
@@ -345,14 +347,14 @@
     q2.wait_recv()
     for copy in g3:
         copy.wait_recv()
-    f2_t = (h2[...] + h2r[...]) + dot3(split(f3[...]), split(e3[...]), NT)
-    f1_half = y1[...] + dot3(split(f2_t), split(e2[...]), NT)
+    f2_t = (h2[...] + h2r[...]) + dot3(split(f3[...]), (et[4], et[5]))
+    f1_half = y1[...] + dot3(split(f2_t), (et[2], et[3]))
     f1[pl.ds(keep, 64), :] = f1_half
     g1 = send(f1.at[pl.ds(keep, 64)], f1.at[pl.ds(keep, 64)], p1)
     near_side(0, v3, 3)
     near_side(1, v3, 3)
     g1.wait_recv()
-    f0 = y0[...] + dot3(split(f1[...]), split(e1[...]), NT)
+    f0 = y0[...] + dot3(split(f1[...]), (et[0], et[1]))
     f0_hi, f0_lo = split(f0.T)
     f0_both = jnp.concatenate([f0_hi, f0_lo], axis=1)
 
@@ -395,7 +397,7 @@
             f32(64, 128), f32(32, 128),
             f32(4, 128, 256), f32(4, 64, 256), f32(4, 64, 128), f32(4, 32, 128),
             f32(64, 256), f32(64, 256), f32(64, 256), f32(3, 16, 256), f32(64, 256),
-            f32(128, 256), f32(128, 256), f32(64, 256),
+            f32(128, 256), f32(128, 256), f32(64, 256), b16(6, 256, 256),
             pltpu.SemaphoreType.DMA((9,)),
             pltpu.SemaphoreType.DMA((copies,)),
             pltpu.SemaphoreType.DMA((copies,)),

time: 57.8 us -> 57.6 us (level)
  no operation moved by 1% of the time
where the time goes in v4:
time: 57.6 us; the launch traced here: 57.3 us
  Pallas kernels  55.4 us (96%)
  local copies, waits for them, and re-layouts  1.87 us (3%)
    pallas_call x1, Pallas kernels, per_device(): pl.pallas_call(kernel, out_shape=jax.ShapeDtypeStruct((LEAF, NCOL), F32),...  55.4 us
    unnamed x1, local copies, waits for them, and re-layouts  1.87 us

profile of v4, /device:TPU:24, one launch (start us, length us, event | category | flops | bytes accessed | tf_op | source)
XLA Modules:
  0.0 57.3 jit_solution(11895593748888993725)
XLA Ops:
  0.0 55.4 %shard_map.73 = f32[1024,128]{1,0:T(8,128)} custom-call(f32[1024,128]{1,0:T(8,128)} %values.1, f32[3,1024]{1,0:T(4,128)} %coords_in.1, s32[1,1024]{1,0:T(1,128)} %bitcast.4, f32[1024,256]{1,0:T(8,128)} %basis.1, f32[448,256]{1,0:T(8,128)} %transfers.1, f32[960,256]{1,0:T(8,128)} %couplings.1, s32[2,4]{1,0:T(2,128)} %bitcast.5), custom_call_target="tpu_custom_call" | custom-call | flops 3221225472 | bytes 4194304 | tf_op jit(solution)/shard_map/pallas_call | solution.py:385
  55.4 1.9 %copy.9 = f32[1024,128]{1,0:T(8,128)} copy(f32[1024,128]{1,0:T(8,128)} %shard_map.73) | data formatting | bytes 1048576

commit v5 on v4

--- a/solution.py
+++ b/solution.py
@@ -303,11 +303,11 @@
     get_cp0.wait()
     y0[...] = dot3(split(both0), split(cp0[...]))
 
-    v1 = share(1)
     s3_up.wait_recv()
     f3_up = relay(r2.at[0], r2.at[1], 4)
     s3_down.wait_recv()
     f3_down = relay(r2.at[2], r2.at[3], -4)
+    v1 = share(1)
     get_cw.wait()
     cw_near.wait_recv()
     for copy in s4:

time: 57.6 us -> 58.8 us (1.021)
  Pallas kernels: 55.4 us -> 56.7 us
    pallas_call x1, Pallas kernels: 55.4 us -> 56.7 us  [per_device(): pl.pallas_call(kernel, out_shape=jax.ShapeDtypeStruct((LEAF, NCOL), F32),...]
where the time goes in v5:
time: 58.8 us; the launch traced here: 58.6 us
  Pallas kernels  56.7 us (96%)
  local copies, waits for them, and re-layouts  1.87 us (3%)
    pallas_call x1, Pallas kernels, per_device(): pl.pallas_call(kernel, out_shape=jax.ShapeDtypeStruct((LEAF, NCOL), F32),...  56.7 us
    unnamed x1, local copies, waits for them, and re-layouts  1.87 us

profile of v5, /device:TPU:24, one launch (start us, length us, event | category | flops | bytes accessed | tf_op | source)
XLA Modules:
  0.0 58.6 jit_solution(13484745822243686223)
XLA Ops:
  0.0 56.7 %shard_map.73 = f32[1024,128]{1,0:T(8,128)} custom-call(f32[1024,128]{1,0:T(8,128)} %values.1, f32[3,1024]{1,0:T(4,128)} %coords_in.1, s32[1,1024]{1,0:T(1,128)} %bitcast.4, f32[1024,256]{1,0:T(8,128)} %basis.1, f32[448,256]{1,0:T(8,128)} %transfers.1, f32[960,256]{1,0:T(8,128)} %couplings.1, s32[2,4]{1,0:T(2,128)} %bitcast.5), custom_call_target="tpu_custom_call" | custom-call | flops 3221225472 | bytes 4194304 | tf_op jit(solution)/shard_map/pallas_call | solution.py:385
  56.7 1.9 %copy.9 = f32[1024,128]{1,0:T(8,128)} copy(f32[1024,128]{1,0:T(8,128)} %shard_map.73) | data formatting | bytes 1048576
